TPU v7x, 32 devices: a whole 2x2x4 slice. The times are simulated.
32 devices in a mesh: dp: 8 (over y, x, core), col: 4 (over z).
Axes of the slice: x: 2, y: 2, z: 4, core: 2. Of those that a mesh axis runs over, the one named last changes fastest.
Arguments:
- activ: bfloat16 [2048, 8192], P('dp'), may hold values from -6 to 6
- grad_out: bfloat16 [2048, 26624], P('dp', 'col'), may hold values from -0.125 to 0.125
- signs: int32 [32768], P('col'), may hold values from -1 to 1, as said below
- kept: int32 [512], replicated, may hold values from 0 to 32767, as said below
Outputs:
- sketch: float32 [8192, 512], P('dp', 'col')
- projection: float32 [512, 26624], P('dp', 'col')
Inputs may be any that keep to these rules, and one draw needn't show every extreme that they name: `signs`: each entry is +1 or -1. `kept`: the 512 indices are distinct.
All inputs are finite; a program needn't handle non-finite values.
Results may differ from a plain program's by a relative error of at most 0.0095.
Values may be sent and summed in bfloat16 or wider, within the bound.
A program may use at most 256 MiB of HBM per device.

v0:
```python
import math

import jax
import jax.numpy as jnp
from jax import lax
from jax.sharding import PartitionSpec as P


def hadamard_table(length):
    row_ids = lax.broadcasted_iota(jnp.int32, (length, length), 0)
    col_ids = lax.broadcasted_iota(jnp.int32, (length, length), 1)
    common = jnp.bitwise_and(row_ids, col_ids)
    parity = jnp.zeros((length, length), jnp.int32)
    for shift_bit in range(max(length.bit_length() - 1, 0)):
        parity = parity + jnp.bitwise_and(jnp.right_shift(common, shift_bit), 1)
    return (1 - 2 * jnp.bitwise_and(parity, 1)).astype(jnp.float32)


def kron_transform(values, length, highest):
    row_count = values.shape[0]
    inner_len = min(length, 128)
    outer_len = length // inner_len
    shaped = values.reshape(row_count, outer_len, inner_len)
    shaped = jnp.einsum("rab,bc->rac", shaped, hadamard_table(inner_len), precision=highest)
    shaped = jnp.einsum("rab,ac->rcb", shaped, hadamard_table(outer_len), precision=highest)
    return shaped.reshape(row_count, length)


def per_device(activ, grad_out, signs, kept):
    dp_count = lax.axis_size("dp")
    col_count = lax.axis_size("col")
    my_col = lax.axis_index("col")
    tok_dev = activ.shape[0]
    row_dev = activ.shape[1] // dp_count
    ff_dev = grad_out.shape[1]
    col_dev = signs.shape[0]
    total_cols = col_dev * col_count
    highest = lax.Precision.HIGHEST
    mine = lax.all_to_all(activ, "dp", split_axis=1, concat_axis=0, tiled=True)
    empty = jnp.zeros((row_dev, ff_dev), jnp.float32)
    piece = lax.all_gather(grad_out, "dp", axis=0, tiled=True)
    group_count = piece.shape[0] // tok_dev

    def one_group(index, acc):
        act_group = lax.dynamic_slice_in_dim(mine, index * tok_dev, tok_dev, 0)
        grad_group = lax.dynamic_slice_in_dim(piece, index * tok_dev, tok_dev, 0)
        partial_grad = lax.dot_general(
            act_group, grad_group, (((0,), (0,)), ((), ())), preferred_element_type=jnp.float32
        )
        rounded = lax.optimization_barrier(partial_grad.astype(jnp.bfloat16))
        return acc + rounded.astype(jnp.float32)

    gradient = lax.fori_loop(0, group_count, one_group, empty)
    padded = jnp.pad(gradient, ((0, 0), (0, col_dev - ff_dev))) * signs.astype(jnp.float32)[None, :]
    scale = 1.0 / math.sqrt(total_cols)
    mixed_cols = kron_transform(padded, col_dev, highest) * scale
    owner_dev = kept // col_dev
    place_col = kept - owner_dev * col_dev
    num_bits = col_count.bit_length() - 1
    picked = jnp.take(mixed_cols, place_col, axis=1)
    common = jnp.bitwise_and(owner_dev, my_col)
    parity = jnp.zeros_like(common)
    for step_bit in range(num_bits):
        parity = parity + jnp.bitwise_and(jnp.right_shift(common, step_bit), 1)
    factor = (1 - 2 * jnp.bitwise_and(parity, 1)).astype(jnp.float32)
    sketch = lax.psum_scatter(picked * factor[None, :], "col", scatter_dimension=1, tiled=True)
    full_rows = lax.all_gather(sketch, "col", axis=1, tiled=True)
    local_gram = jnp.dot(full_rows.T, full_rows, precision=highest)
    gram_matrix = lax.psum(local_gram, "dp")
    keep_count = gram_matrix.shape[0]
    shift_size = 0.05 * jnp.trace(gram_matrix) / keep_count
    shifted = gram_matrix + shift_size * jnp.eye(keep_count, dtype=jnp.float32)
    chol_factor = jnp.linalg.cholesky(shifted)
    basis_rows = jax.scipy.linalg.solve_triangular(chol_factor, full_rows.T, lower=True).T
    projection = lax.psum_scatter(
        lax.dot_general(
            basis_rows,
            gradient,
            (((0,), (0,)), ((), ())),
            precision=highest,
            preferred_element_type=jnp.float32,
        ),
        "dp",
        scatter_dimension=0,
        tiled=True,
    )
    return (sketch, projection)


def solution(mesh):
    placed = (P("dp", None), P("dp", "col"), P("col"), P())
    return jax.shard_map(
        per_device,
        mesh=mesh,
        in_specs=placed,
        out_specs=(P("dp", "col"), P("dp", "col")),
        check_vma=False,
    )
```

profile of v0, /device:TPU:0, one launch (start us, length us, event | category | flops | bytes accessed | tf_op | source)
XLA Modules:
  0.0 1066.4 jit_solution(4597313105411401098)
XLA Ops:
  19.9 83.9 %all-to-all-done = bf16[256,8,1024]{2,0,1:T(8,128)(2,1)} async-done(((bf16[256,8,1024]{2,0,1:T(8,128)(2,1)}), bf16[256,8,1024]{2,0,1:T(8,128)(2,1)}, u32[]{:S(2)}, u32[]{:S(2)}) %all-to-all-start) | async-done | bytes 4194336 | tf_op jit(solution)/shard_map/all_to_all | solution.py:39
  103.8 83.9 %all-gather.3.cloned.1.call-done = bf16[2048,6656]{1,0:T(8,128)(2,1)} async-done(((bf16[256,6656]{1,0:T(8,128)(2,1)}), bf16[2048,6656]{1,0:T(8,128)(2,1)}) %all-gather.3.cloned.1.call-update) | async-done | bytes 27262992 | tf_op jit(solution)/shard_map/all_gather | solution.py:41
  187.7 268.0 %while.16 = (s32[]{:T(128)}, f32[1024,6656]{1,0:T(8,128)}, bf16[2048,1024]{1,0:T(8,128)(2,1)}, bf16[2048,6656]{1,0:T(8,128)(2,1)}, s32[]{:T(128)}, /*index=5*/s32[]{:T(128)}, s32[]{:T(128)}, s32[]{:T(128)}) while((s32[]{:T(128)}, f32[1024,6656]{1,0:T(8,128)}, bf16[2048,1024]{1,0:T(8,128)(2,1)}, bf16[2048,6656]{1,0:T(8,128)(2,1)}, ...), condition=%wide.region_1.0_spmd.clone, body=%wide.region_0.0_spmd.clone.sunk | while | flops 3516923904 | bytes 85722248 | solution.py:53
  187.7 10.7 %convolution_convert_fusion.2 = bf16[1024,6656]{1,0:T(8,128)(2,1)} fusion(bf16[2048,6656]{1,0:T(8,128)(2,1)} %get-tuple-element.212, s32[]{:T(128)S(6)} %select_n.49, bf16[2048,1024]{1,0:T(8,128)(2,1)} %get-tuple-element.211), kind=kOutput, calls=%fused_computation.4.clone.1 | convolution fusion | flops 3496476672 | bytes 17564672 | tf_op jit(solution)/shard_map/while/body/eval_jaxpr/dot_general | solution.py:47
  198.4 15.3 %select_add_fusion.3 = f32[1024,6656]{1,0:T(8,128)} fusion(f32[1024,6656]{1,0:T(8,128)} %get-tuple-element.202, bf16[1024,6656]{1,0:T(8,128)(2,1)} %convolution_convert_fusion.2, pred[]{:T(512)S(6)} %compare.49), kind=kLoop, calls=%fused_computation.3.clone.1 | loop fusion | flops 20447232 | bytes 68157440 | tf_op jit(solution)/shard_map/while/body/eval_jaxpr/add | solution.py:51
  213.7 10.7 %convolution_convert_fusion.2 = bf16[1024,6656]{1,0:T(8,128)(2,1)} fusion(bf16[2048,6656]{1,0:T(8,128)(2,1)} %get-tuple-element.212, s32[]{:T(128)S(6)} %select_n.49, bf16[2048,1024]{1,0:T(8,128)(2,1)} %get-tuple-element.211), kind=kOutput, calls=%fused_computation.4.clone.1 | convolution fusion | flops 3496476672 | bytes 17564672 | tf_op jit(solution)/shard_map/while/body/eval_jaxpr/dot_general | solution.py:47
  224.4 23.9 %select_add_fusion.3 = f32[1024,6656]{1,0:T(8,128)} fusion(f32[1024,6656]{1,0:T(8,128)} %get-tuple-element.202, bf16[1024,6656]{1,0:T(8,128)(2,1)} %convolution_convert_fusion.2, pred[]{:T(512)S(6)} %compare.49), kind=kLoop, calls=%fused_computation.3.clone.1 | loop fusion | flops 20447232 | bytes 68157440 | tf_op jit(solution)/shard_map/while/body/eval_jaxpr/add | solution.py:51
  248.3 10.7 %convolution_convert_fusion.2 = bf16[1024,6656]{1,0:T(8,128)(2,1)} fusion(bf16[2048,6656]{1,0:T(8,128)(2,1)} %get-tuple-element.212, s32[]{:T(128)S(6)} %select_n.49, bf16[2048,1024]{1,0:T(8,128)(2,1)} %get-tuple-element.211), kind=kOutput, calls=%fused_computation.4.clone.1 | convolution fusion | flops 3496476672 | bytes 17564672 | tf_op jit(solution)/shard_map/while/body/eval_jaxpr/dot_general | solution.py:47
  259.0 23.9 %select_add_fusion.3 = f32[1024,6656]{1,0:T(8,128)} fusion(f32[1024,6656]{1,0:T(8,128)} %get-tuple-element.202, bf16[1024,6656]{1,0:T(8,128)(2,1)} %convolution_convert_fusion.2, pred[]{:T(512)S(6)} %compare.49), kind=kLoop, calls=%fused_computation.3.clone.1 | loop fusion | flops 20447232 | bytes 68157440 | tf_op jit(solution)/shard_map/while/body/eval_jaxpr/add | solution.py:51
  293.6 23.9 %select_add_fusion.3 = f32[1024,6656]{1,0:T(8,128)} fusion(f32[1024,6656]{1,0:T(8,128)} %get-tuple-element.202, bf16[1024,6656]{1,0:T(8,128)(2,1)} %convolution_convert_fusion.2, pred[]{:T(512)S(6)} %compare.49), kind=kLoop, calls=%fused_computation.3.clone.1 | loop fusion | flops 20447232 | bytes 68157440 | tf_op jit(solution)/shard_map/while/body/eval_jaxpr/add | solution.py:51
  317.4 10.7 %convolution_convert_fusion.2 = bf16[1024,6656]{1,0:T(8,128)(2,1)} fusion(bf16[2048,6656]{1,0:T(8,128)(2,1)} %get-tuple-element.212, s32[]{:T(128)S(6)} %select_n.49, bf16[2048,1024]{1,0:T(8,128)(2,1)} %get-tuple-element.211), kind=kOutput, calls=%fused_computation.4.clone.1 | convolution fusion | flops 3496476672 | bytes 17564672 | tf_op jit(solution)/shard_map/while/body/eval_jaxpr/dot_general | solution.py:47
  328.1 23.9 %select_add_fusion.3 = f32[1024,6656]{1,0:T(8,128)} fusion(f32[1024,6656]{1,0:T(8,128)} %get-tuple-element.202, bf16[1024,6656]{1,0:T(8,128)(2,1)} %convolution_convert_fusion.2, pred[]{:T(512)S(6)} %compare.49), kind=kLoop, calls=%fused_computation.3.clone.1 | loop fusion | flops 20447232 | bytes 68157440 | tf_op jit(solution)/shard_map/while/body/eval_jaxpr/add | solution.py:51
  362.7 23.9 %select_add_fusion.3 = f32[1024,6656]{1,0:T(8,128)} fusion(f32[1024,6656]{1,0:T(8,128)} %get-tuple-element.202, bf16[1024,6656]{1,0:T(8,128)(2,1)} %convolution_convert_fusion.2, pred[]{:T(512)S(6)} %compare.49), kind=kLoop, calls=%fused_computation.3.clone.1 | loop fusion | flops 20447232 | bytes 68157440 | tf_op jit(solution)/shard_map/while/body/eval_jaxpr/add | solution.py:51
  397.2 23.9 %select_add_fusion.3 = f32[1024,6656]{1,0:T(8,128)} fusion(f32[1024,6656]{1,0:T(8,128)} %get-tuple-element.202, bf16[1024,6656]{1,0:T(8,128)(2,1)} %convolution_convert_fusion.2, pred[]{:T(512)S(6)} %compare.49), kind=kLoop, calls=%fused_computation.3.clone.1 | loop fusion | flops 20447232 | bytes 68157440 | tf_op jit(solution)/shard_map/while/body/eval_jaxpr/add | solution.py:51
  431.8 23.9 %select_add_fusion.3 = f32[1024,6656]{1,0:T(8,128)} fusion(f32[1024,6656]{1,0:T(8,128)} %get-tuple-element.202, bf16[1024,6656]{1,0:T(8,128)(2,1)} %convolution_convert_fusion.2, pred[]{:T(512)S(6)} %compare.49), kind=kLoop, calls=%fused_computation.3.clone.1 | loop fusion | flops 20447232 | bytes 68157440 | tf_op jit(solution)/shard_map/while/body/eval_jaxpr/add | solution.py:51
  455.7 11.2 %multiply_bitcast_fusion.1 = f32[128,8,64,128]{3,1,2,0:T(8,128)S(1)} fusion(f32[1024,6656]{1,0:T(8,128)} %get-tuple-element.81, f32[8192]{0:T(1024)S(1)} %convert_element_type.30), kind=kLoop, calls=%fused_computation.9 | loop fusion | flops 8388608 | bytes 60850176
  466.9 12.2 %copy.25 = f32[128,8,64,128]{3,2,1,0:T(8,128)} copy(f32[128,8,64,128]{3,1,2,0:T(8,128)S(1)} %multiply_bitcast_fusion.1) | data formatting | bytes 67108864
  479.1 32.6 %fusion.43 = f32[1024,64,128]{2,1,0:T(8,128)} fusion(f32[1024,64,128]{2,1,0:T(8,128)} %bitcast.77), kind=kOutput, calls=%fused_computation.67 | convolution fusion | flops 12885311488 | bytes 67108864 | tf_op jit(solution)/shard_map/rab,bc->rac/dot_general | solution.py:24
  511.7 37.6 %multiply_bitcast_fusion = f32[1024,64,128]{2,1,0:T(8,128)} fusion(f32[1024,64,128]{2,1,0:T(8,128)} %fusion.43), kind=kOutput, calls=%fused_computation.8 | convolution fusion | flops 6450929664 | bytes 67108864 | tf_op jit(solution)/shard_map/rab,ac->rcb/dot_general | solution.py:25
  549.4 32.2 %copy.22 = f32[1024,64,128]{0,2,1:T(8,128)} copy(f32[1024,64,128]{2,1,0:T(8,128)} %multiply_bitcast_fusion) | data formatting | bytes 67108864 | tf_op jit(solution)/shard_map/mul | solution.py:56
  581.5 13.4 %gather_fusion = f32[512,1024]{1,0:T(8,128)S(1)} fusion(f32[1024,8192]{0,1:T(8,128)} %bitcast.78, s32[1024]{0:T(1024)S(1)} %copy-done.6), kind=kCustom, calls=%fused_computation | custom fusion | bytes 4196352 | tf_op jit(solution)/shard_map/jit(_take)/gather | solution.py:60
  596.6 44.0 %reduce-scatter.3.cloned.1.call-done = f32[1024,128]{0,1:T(8,128)} async-done(((f32[1024,512]{0,1:T(8,128)}), f32[1024,128]{0,1:T(8,128)}) %reduce-scatter.3.cloned.1.call-update) | async-done | bytes 524304 | tf_op jit(solution)/shard_map/reduce_scatter | solution.py:66
  640.6 46.9 %all-gather.5.cloned.1.call-done = f32[1024,512]{0,1:T(8,128)} async-done(((f32[1024,128]{0,1:T(8,128)}), f32[1024,512]{0,1:T(8,128)}) %all-gather.5.cloned.1.call-update) | async-done | bytes 2097168 | tf_op jit(solution)/shard_map/all_gather | solution.py:67
  703.1 46.7 %all-reduce.4.cloned.1.call-done = f32[512,512]{0,1:T(8,128)} async-done(((f32[512,512]{0,1:T(8,128)}), f32[512,512]{0,1:T(8,128)}) %all-reduce.4.cloned.1.call-update) | async-done | bytes 1048592 | tf_op jit(solution)/shard_map/psum | solution.py:69
  754.3 11.7 %cholesky.95 = f32[128,128]{1,0:T(8,128)S(1)} custom-call(f32[128,128]{1,0:T(8,128)S(1)} %cholesky.247), custom_call_target="Cholesky" | custom-call | tf_op jit(solution)/shard_map/jit(cholesky)/cholesky | solution.py:73
  776.6 11.7 %cholesky.199 = f32[128,128]{1,0:T(8,128)S(1)} custom-call(f32[128,128]{1,0:T(8,128)S(1)} %cholesky.251), custom_call_target="Cholesky" | custom-call | tf_op jit(solution)/shard_map/jit(cholesky)/cholesky | solution.py:73
  805.0 11.7 %cholesky.220 = f32[128,128]{1,0:T(8,128)S(1)} custom-call(f32[128,128]{1,0:T(8,128)S(1)} %cholesky.256), custom_call_target="Cholesky" | custom-call | tf_op jit(solution)/shard_map/jit(cholesky)/cholesky | solution.py:73
  828.3 12.1 %cholesky.237 = f32[128,128]{1,0:T(8,128)S(1)} custom-call(f32[128,128]{1,0:T(8,128)S(1)} %convolution_subtract_fusion.4), custom_call_target="Cholesky" | custom-call | tf_op jit(solution)/shard_map/jit(cholesky)/cholesky | solution.py:73
  846.1 14.3 %while.15 = (s32[]{:T(128)}, f32[512,512]{0,1:T(8,128)}, s32[4,2]{0,1:T(2,128)S(1)}, f32[4,128,128]{2,1,0:T(8,128)}, s32[]{:T(128)}) while((s32[]{:T(128)}, f32[512,512]{0,1:T(8,128)}, s32[4,2]{0,1:T(2,128)S(1)}, f32[4,128,128]{2,1,0:T(8,128)}, s32[]{:T(128)}) %tuple.60), condition=%wide.while_cond, body=%wide.while_body.sunk | while | flops 2 | bytes 393829 | solution.py:74
  860.4 40.1 %custom-call.34 = f32[4,128,128]{1,2,0:T(8,128)S(1)} custom-call(f32[4,128,128]{2,1,0:T(8,128)} %get-tuple-element.89), custom_call_target="InvertDiagBlocksLowerTriangular" | custom-call | tf_op jit(solution)/shard_map/jit(_solve_triangular)/triangular_solve | solution.py:74
  908.4 54.1 %fusion.3 = f32[512,6656]{1,0:T(8,128)} fusion(f32[1024,6656]{1,0:T(8,128)} %get-tuple-element.81, f32[128,1024]{1,0:T(8,128)S(1)} %fusion.34, f32[128,1024]{1,0:T(8,128)} %copy-done.4, f32[128,1024]{1,0:T(8,128)S(1)} %fusion.37, f32[128,1024]{1,0:T(8,128)S(1)} %fusion.24), kind=kOutput, calls=%fused_computation.11 | convolution fusion | flops 41877504000 | bytes 42991616 | tf_op jit(solution)/shard_map/dot_general | solution.py:76
  964.5 95.2 %reduce-scatter.5.cloned.1.call-done = f32[64,6656]{1,0:T(8,128)} async-done(((f32[512,6656]{1,0:T(8,128)}), f32[64,6656]{1,0:T(8,128)}) %reduce-scatter.5.cloned.1.call-update) | async-done | bytes 1703952 | tf_op jit(solution)/shard_map/reduce_scatter | solution.py:75
  (108 shorter events, 142.6 us)
Async XLA Ops:
  7.2 180.6 %all-gather.3.cloned.1.call-start = ((), (), s32[]{:S(2)}) async-start(), calls=%async_computation.3 | async-start | bytes 30670848 | tf_op jit(solution)/shard_map/all_gather | solution.py:41
  12.8 5.4 copy-start.5
  12.8 5.4 copy-start.8
  12.8 91.0 %all-to-all-start = ((bf16[256,8,1024]{2,0,1:T(8,128)(2,1)}), bf16[256,8,1024]{2,0,1:T(8,128)(2,1)}, u32[]{:S(2)}, u32[]{:S(2)}) async-start(bf16[256,8,1024]{2,0,1:T(8,128)(2,1)} %bitcast.83), calls=%async_computation | async-start | bytes 8388608 | tf_op jit(solution)/shard_map/all_to_all | solution.py:39
  18.1 622.5 %reduce-scatter.3.cloned.1.call-start = ((), (), s32[]{:S(2)}) async-start(), calls=%async_computation.4 | async-start | bytes 2621440 | tf_op jit(solution)/shard_map/reduce_scatter | solution.py:66
  549.4 32.2 %copy-start.6 = (s32[1024]{0:T(1024)S(1)}, s32[1024]{0:T(1024)}, u32[]{:S(2)}) copy-start(s32[1024]{0:T(1024)} %pad_clamp_fusion) | copy-start | bytes 12292
  581.5 13.4 %copy-start.7 = (f32[512]{0:T(512)S(1)}, f32[512]{0:T(512)}, u32[]{:S(2)}) copy-start(f32[512]{0:T(512)} %subtract_convert_fusion) | copy-start | bytes 6148
  581.5 13.4 %copy-start.9 = (pred[512]{0:T(512)(128)(4,1)S(1)}, pred[512]{0:T(512)(128)(4,1)}, u32[]{:S(2)}) copy-start(pred[512]{0:T(512)(128)(4,1)} %get-tuple-element.127) | copy-start | bytes 1540
  596.6 91.0 %all-gather.5.cloned.1.call-start = ((), (), s32[]{:S(2)}) async-start(), calls=%async_computation.5 | async-start | bytes 2621440 | tf_op jit(solution)/shard_map/all_gather | solution.py:67
  640.6 109.1 %all-reduce.4.cloned.1.call-start = ((), (), s32[]{:S(2)}) async-start(), calls=%async_computation.6 | async-start | bytes 2097152 | tf_op jit(solution)/shard_map/psum | solution.py:69
  694.3 365.5 %reduce-scatter.5.cloned.1.call-start = ((), (), s32[]{:S(2)}) async-start(), calls=%async_computation.7 | async-start | bytes 15335424 | tf_op jit(solution)/shard_map/reduce_scatter | solution.py:75
  749.7 4.3 copy-start.1
  754.3 34.7 %copy-start.2 = (f32[512,512]{1,0:T(8,128)}, f32[512,512]{1,0:T(8,128)S(1)}, u32[]{:S(2)}) copy-start(f32[512,512]{1,0:T(8,128)S(1)} %fusion.23) | copy-start | bytes 3145732
  789.2 111.3 %copy-start = (f32[1024,512]{0,1:T(8,128)S(1)}, f32[1024,512]{0,1:T(8,128)}, u32[]{:S(2)}) copy-start(f32[1024,512]{0,1:T(8,128)} %all-gather.5.cloned.1.call-done) | copy-start | bytes 6291460
  905.5 2.2 copy-start.4
  962.5 1.0 copy-start.3
Sparse Core Ops, SparseCore 0:
  9.9 177.7 all-gather.2
  596.7 43.8 reduce-scatter.2
  642.2 45.2 all-gather.4
  694.4 55.3 all-reduce.3
  962.7 97.0 reduce-scatter.4
where the time goes:
time: 1080 us; the launch traced here: 1070 us
  waiting for transfers between devices  401 us (37%)
  other arithmetic  321 us (30%)
  matrix products  229 us (21%)
  local copies, waits for them, and re-layouts  82.8 us (8%)
  between operations  17.5 us (2%)
  starting transfers between devices  14.2 us (1%)
    add x8, other arithmetic, one_group(): return acc + rounded.astype(jnp.float32)  182 us
    reduce_scatter x1, waiting for transfers between devices, per_device(): lax.psum_scatter(lax.dot_general(basis_rows, gradient, (((0,), (0,)), (()...  95.2 us
    dot_general x8, matrix products, one_group(): lax.dot_general(act_group, grad_group, (((0,), (0,)), ((), ())), preferre...  85.5 us
    all_gather x1, waiting for transfers between devices, per_device(): piece = lax.all_gather(grad_out, 'dp', axis=0, tiled=True)  83.9 us
    all_to_all x1, waiting for transfers between devices, per_device(): mine = lax.all_to_all(activ, 'dp', split_axis=1, concat_axis=0, tiled=True)  83.9 us
    another operation x14, other arithmetic, per_device(): chol_factor = jnp.linalg.cholesky(shifted)  79.5 us
    dot_general x1, matrix products, per_device(): lax.dot_general(basis_rows, gradient, (((0,), (0,)), ((), ())), precision...  54.1 us
    all_gather x1, waiting for transfers between devices, per_device(): full_rows = lax.all_gather(sketch, 'col', axis=1, tiled=True)  46.9 us
  transfers between devices with their start and end apart: 6, of which 6 were waited for; matrix products, arithmetic and copies ran while one was open for 1% of the time, Pallas kernels for 0%

commit v1 on v0

v1 whole, which is shorter than its diff:
```python
import math

import jax
import jax.numpy as jnp
from jax import lax
from jax.experimental import pallas as pl
from jax.experimental.pallas import tpu as pltpu
from jax.sharding import PartitionSpec as P

HI = lax.Precision.HIGHEST


def dot_hi(left, right, dims):
    return lax.dot_general(left, right, (dims, ((), ())), precision=HI,
                           preferred_element_type=jnp.float32)


def factor_block(both_ref):
    size = both_ref.shape[0]
    lane = lax.broadcasted_iota(jnp.int32, (8, size), 1)
    sub = lax.broadcasted_iota(jnp.int32, (8, size), 0)

    for p in range(size // 8):
        lo = 8 * p
        rows = both_ref[lo:lo + 8, :]
        rw, rv = rows[:, :size], rows[:, size:]
        cols = [jnp.broadcast_to(rw[:, lo + a:lo + a + 1], (8, size)) for a in range(8)]
        for a in range(8):
            pivot = jnp.broadcast_to(cols[a][a:a + 1, :], (8, size))
            root = lax.rsqrt(pivot)
            mult = jnp.where(sub > a, cols[a] * (root * root), jnp.where(sub == a, 1.0 - root, 0.0))
            for b in range(a + 1, 8):
                cols[b] = cols[b] - mult * jnp.broadcast_to(cols[b][a:a + 1, :], (8, size))
            rw = rw - mult * jnp.broadcast_to(rw[a:a + 1, :], (8, size))
            rv = rv - mult * jnp.broadcast_to(rv[a:a + 1, :], (8, size))
        done = jnp.concatenate([rw, rv], axis=1)
        both_ref[lo:lo + 8, :] = done
        if lo + 8 < size:
            left = jnp.where(lane >= lo + 8, rw, 0.0)
            step = dot_hi(left, done, ((0,), (0,)))
            both_ref[lo + 8:, :] = both_ref[lo + 8:, :] - step[lo + 8:, :]


def inverse_factor_kernel(gram_ref, out_ref, work, both):
    count = gram_ref.shape[0]
    size = both.shape[0]
    blocks = count // size
    row = lax.broadcasted_iota(jnp.int32, (count, count), 0)
    col = lax.broadcasted_iota(jnp.int32, (count, count), 1)
    gram = gram_ref[...]
    trace = jnp.sum(jnp.where(row == col, gram, 0.0))
    work[...] = gram + jnp.where(row == col, 0.05 * trace / count, 0.0)
    out_ref[...] = jnp.zeros_like(out_ref)
    eye = (lax.broadcasted_iota(jnp.int32, (size, size), 0)
           == lax.broadcasted_iota(jnp.int32, (size, size), 1)).astype(jnp.float32)
    for k in range(blocks):
        lo, hi = k * size, (k + 1) * size
        both[:, :size] = work[lo:hi, lo:hi]
        both[:, size:] = eye
        factor_block(both)
        inv = both[:, size:]
        if k:
            out_ref[lo:hi, :lo] = dot_hi(inv, out_ref[lo:hi, :lo], ((1,), (0,)))
        out_ref[lo:hi, lo:hi] = inv
        if hi < count:
            panel = dot_hi(inv, work[lo:hi, hi:], ((1,), (0,)))
            work[hi:, hi:] = work[hi:, hi:] - dot_hi(panel, panel, ((0,), (0,)))
            out_ref[hi:, :hi] = out_ref[hi:, :hi] - dot_hi(panel, out_ref[lo:hi, :hi], ((0,), (0,)))


def inverse_factor(gram):
    count = gram.shape[0]
    size = 128
    return pl.pallas_call(
        inverse_factor_kernel,
        out_shape=jax.ShapeDtypeStruct((count, count), jnp.float32),
        in_specs=[pl.BlockSpec(memory_space=pltpu.VMEM)],
        out_specs=pl.BlockSpec(memory_space=pltpu.VMEM),
        scratch_shapes=[pltpu.VMEM((count, count), jnp.float32),
                        pltpu.VMEM((size, 2 * size), jnp.float32)],
        compiler_params=pltpu.CompilerParams(vmem_limit_bytes=32 * 1024 * 1024),
        cost_estimate=pl.CostEstimate(flops=10**9, bytes_accessed=2 * 10**6, transcendentals=4096),
    )(gram)


def parity_sign(common, num_bits):
    parity = jnp.zeros_like(common)
    for shift_bit in range(num_bits):
        parity = parity + jnp.bitwise_and(jnp.right_shift(common, shift_bit), 1)
    return (1 - 2 * jnp.bitwise_and(parity, 1)).astype(jnp.bfloat16)


def kept_columns(signs, kept, my_col, ff_dev, col_dev, total_cols):
    num_bits = total_cols.bit_length() - 1
    inner = math.gcd(ff_dev, 128)
    outer = ff_dev // inner
    start = my_col * col_dev + inner * lax.broadcasted_iota(jnp.int32, (outer, 1), 0)
    high = parity_sign(jnp.bitwise_and(start, kept[None, :]), num_bits)
    place = lax.broadcasted_iota(jnp.int32, (inner, 1), 0)
    low = parity_sign(jnp.bitwise_and(place, kept[None, :]), num_bits)
    own = signs[:ff_dev].astype(jnp.bfloat16).reshape(outer, inner, 1)
    return (high[:, None, :] * low[None, :, :] * own).reshape(ff_dev, kept.shape[0])


def split(values):
    top = values.astype(jnp.bfloat16)
    return top, (values - top.astype(jnp.float32)).astype(jnp.bfloat16)


def dot_f32(left, right, dims):
    return lax.dot_general(left, right, (dims, ((), ())), preferred_element_type=jnp.float32)


def per_device(activ, grad_out, signs, kept):
    col_count = lax.axis_size("col")
    my_col = lax.axis_index("col")
    ff_dev = grad_out.shape[1]
    col_dev = signs.shape[0]
    total_cols = col_dev * col_count
    highest = lax.Precision.HIGHEST
    mine = lax.all_to_all(activ, "dp", split_axis=1, concat_axis=0, tiled=True)
    columns = kept_columns(signs, kept, my_col, ff_dev, col_dev, total_cols)
    mixed = dot_f32(grad_out, columns, ((1,), (0,))) * (1.0 / math.sqrt(total_cols))
    mixed = lax.psum_scatter(mixed, "col", scatter_dimension=1, tiled=True)
    mixed = lax.all_gather(mixed, "dp", axis=0, tiled=True)
    top, rest = split(mixed)
    sketch = dot_f32(mine, top, ((0,), (0,))) + dot_f32(mine, rest, ((0,), (0,)))
    full_rows = lax.all_gather(sketch, "col", axis=1, tiled=True)
    gram_matrix = lax.psum(jnp.dot(full_rows.T, full_rows, precision=highest), "dp")
    top, rest = split(sketch)
    back = dot_f32(mine, top, ((1,), (0,))) + dot_f32(mine, rest, ((1,), (0,)))
    back = lax.psum_scatter(back, "dp", scatter_dimension=0, tiled=True)
    back = lax.all_gather(back, "col", axis=1, tiled=True)
    solved = dot_hi(inverse_factor(gram_matrix), back, ((1,), (1,)))
    top, rest = split(solved)
    part = dot_f32(top, grad_out, ((1,), (0,))) + dot_f32(rest, grad_out, ((1,), (0,)))
    projection = lax.psum_scatter(
        part.astype(jnp.bfloat16), "dp", scatter_dimension=0, tiled=True
    ).astype(jnp.float32)
    return (sketch, projection)


def solution(mesh):
    placed = (P("dp", None), P("dp", "col"), P("col"), P())
    return jax.shard_map(
        per_device,
        mesh=mesh,
        in_specs=placed,
        out_specs=(P("dp", "col"), P("dp", "col")),
        check_vma=False,
    )
```

time: 1080 us -> 348 us (0.32); the launches traced: 1070 us -> 347 us
  other arithmetic: 321 us -> 6.96 us
  matrix products: 229 us -> 29.8 us
  waiting for transfers between devices: 401 us -> 218 us
  local copies, waits for them, and re-layouts: 82.8 us -> 17 us
  Pallas kernels: 0 us -> 38.1 us
  blocking collectives: 0 us -> 17.4 us
    dot_general x12 -> x9, matrix products: 217 us -> 29.8 us  [the longest x7 21.1 us: dot_f32(): lax.dot_general(left, right, (dims, ((), ())), preferred_element_type=jnp...]
    add x9 -> x1, other arithmetic: 184 us -> 0.01 us  [kept_columns(): my_col * col_dev + inner * lax.broadcasted_iota(jnp.int32, (outer, 1), 0)]
    another operation x17 -> x1, other arithmetic: 121 us -> 0.01 us  [the longest x14 79.5 us: per_device(): chol_factor = jnp.linalg.cholesky(shifted)]
    all_gather x1, waiting for transfers between devices: 83.9 us -> 0.01 us  [per_device(): mixed = lax.all_gather(mixed, 'dp', axis=0, tiled=True)]
    all_to_all x1, waiting for transfers between devices: 83.9 us -> 19.1 us  [per_device(): mine = lax.all_to_all(activ, 'dp', split_axis=1, concat_axis=0, tiled=True)]
    pallas_call x0 -> x1, Pallas kernels: none -> 38.1 us  [inverse_factor(): pl.pallas_call(inverse_factor_kernel, out_shape=jax.ShapeDtypeStruct((cou...]
    mul x1 -> x0, local copies, waits for them, and re-layouts: 32.2 us -> none  [per_device(): mixed_cols = kron_transform(padded, col_dev, highest) * scale]
    reduce_scatter x2 -> x3, waiting for transfers between devices: 139 us -> 116 us  [the longest x1 61.4 us: per_device(): lax.psum_scatter(part.astype(jnp.bfloat16), 'dp', scatter_dimension=0, ti...]
  transfers between devices with their start and end apart: 6 -> 7, of which waited for: 6 -> 6; matrix products, arithmetic and copies ran while one was open for 1% -> 8% of each run, Pallas kernels for 0% -> 0%
where the time goes in v1:
time: 348 us; the launch traced here: 347 us
  waiting for transfers between devices  218 us (63%)
  Pallas kernels  38.1 us (11%)
  matrix products  29.8 us (9%)
  blocking collectives  17.4 us (5%)
  local copies, waits for them, and re-layouts  17 us (5%)
  between operations  14.3 us (4%)
  other arithmetic  6.96 us (2%)
  starting transfers between devices  5.72 us (2%)
    reduce_scatter x1, waiting for transfers between devices, per_device(): lax.psum_scatter(part.astype(jnp.bfloat16), 'dp', scatter_dimension=0, ti...  61.4 us
    psum x1, waiting for transfers between devices, per_device(): lax.psum(jnp.dot(full_rows.T, full_rows, precision=highest), 'dp')  42.8 us
    all_gather x1, waiting for transfers between devices, per_device(): full_rows = lax.all_gather(sketch, 'col', axis=1, tiled=True)  39.5 us
    pallas_call x1, Pallas kernels, inverse_factor(): pl.pallas_call(inverse_factor_kernel, out_shape=jax.ShapeDtypeStruct((cou...  38.1 us
    reduce_scatter x1, waiting for transfers between devices, per_device(): back = lax.psum_scatter(back, 'dp', scatter_dimension=0, tiled=True)  31 us
    reduce_scatter x1, waiting for transfers between devices, per_device(): mixed = lax.psum_scatter(mixed, 'col', scatter_dimension=1, tiled=True)  24 us
    dot_general x7, matrix products, dot_f32(): lax.dot_general(left, right, (dims, ((), ())), preferred_element_type=jnp...  21.1 us
    all_to_all x1, waiting for transfers between devices, per_device(): mine = lax.all_to_all(activ, 'dp', split_axis=1, concat_axis=0, tiled=True)  19.1 us
  transfers between devices with their start and end apart: 7, of which 6 were waited for; matrix products, arithmetic and copies ran while one was open for 8% of the time, Pallas kernels for 0%

profile of v1, /device:TPU:0, one launch (start us, length us, event | category | flops | bytes accessed | tf_op | source)
XLA Modules:
  0.0 347.1 jit_solution(15206615442244749762)
XLA Ops:
  7.2 6.6 %copy.8 = bf16[256,8192]{0,1:T(8,128)(2,1)} copy(bf16[256,8192]{1,0:T(8,128)(2,1)} %param.4) | data formatting | bytes 8388608 | tf_op args[0]
  13.7 5.3 %all-to-all-start = ((bf16[256,8,1024]{0,2,1:T(8,128)(2,1)}), bf16[256,8,1024]{0,2,1:T(8,128)(2,1)}, u32[]{:S(2)}, u32[]{:S(2)}) async-start(bf16[256,8,1024]{0,2,1:T(8,128)(2,1)} %bitcast.27), calls=%async_computation.1 | async-start | bytes 8388608 | tf_op jit(solution)/shard_map/all_to_all | solution.py:121
  19.1 0.4 subtract_convert_fusion.6
  19.6 0.3 fusion.44
  19.8 0.4 broadcast_multiply_fusion
  20.3 3.4 bitcast_multiply_fusion
  23.7 2.8 fusion.1
  26.5 24.0 %reduce-scatter.4.cloned.1.call-done = f32[256,128]{0,1:T(8,128)} async-done(((f32[256,512]{0,1:T(8,128)}), f32[256,128]{0,1:T(8,128)}) %reduce-scatter.4.cloned.1.call-update) | async-done | bytes 131088 | tf_op jit(solution)/shard_map/reduce_scatter | solution.py:124
  50.6 19.1 %all-to-all-done = bf16[256,8,1024]{0,2,1:T(8,128)(2,1)} async-done(((bf16[256,8,1024]{0,2,1:T(8,128)(2,1)}), bf16[256,8,1024]{0,2,1:T(8,128)(2,1)}, u32[]{:S(2)}, u32[]{:S(2)}) %all-to-all-start) | async-done | bytes 4194336 | tf_op jit(solution)/shard_map/all_to_all | solution.py:121
  69.7 6.5 %copy.9 = bf16[8,256,1024]{2,1,0:T(8,128)(2,1)} copy(bf16[8,256,1024]{1,2,0:T(8,128)(2,1)} %bitcast.3) | data formatting | bytes 8388608 | tf_op jit(solution)/shard_map/all_to_all | solution.py:121
  76.1 3.4 fusion.4
  79.5 0.4 copy-done.2
  79.9 0.3 copy-done.5
  80.2 1.6 fusion.2
  81.8 0.0 reduce-scatter.6.cloned.1.call-start
  81.8 4.0 %fusion.10 = f32[128,2048]{1,0:T(8,128)S(1)} fusion(bf16[2048,1024]{1,0:T(8,128)(2,1)} %bitcast.24, f32[1024,128]{0,1:T(8,128)} %fusion.2), kind=kOutput, calls=%fused_computation.35 | convolution fusion | flops 537001984 | bytes 5767168 | tf_op jit(solution)/shard_map/dot_general | solution.py:111
  85.9 2.5 fusion
  88.4 0.2 all-reduce.2.cloned.1.call-start
  88.6 39.5 %all-gather.5.cloned.1.call-done = f32[1024,512]{0,1:T(8,128)} async-done(((f32[1024,128]{0,1:T(8,128)}), f32[1024,512]{0,1:T(8,128)}) %all-gather.5.cloned.1.call-update) | async-done | bytes 2097168 | tf_op jit(solution)/shard_map/all_gather | solution.py:128
  128.1 6.7 %fusion.45 = f32[512,512]{1,0:T(8,128)} fusion(f32[1024,512]{0,1:T(8,128)} %all-gather.5.cloned.1.call-done), kind=kOutput, calls=%fused_computation.72 | convolution fusion | flops 3221225472 | bytes 3145728 | tf_op jit(solution)/shard_map/dot_general | solution.py:129
  134.9 0.0 reduce-scatter.8.cloned.1.call-start
  134.9 31.0 %reduce-scatter.6.cloned.1.call-done = f32[256,128]{0,1:T(8,128)} async-done(((f32[2048,128]{0,1:T(8,128)}), f32[256,128]{0,1:T(8,128)}) %reduce-scatter.6.cloned.1.call-update) | async-done | bytes 131088 | tf_op jit(solution)/shard_map/reduce_scatter | solution.py:132
  165.9 17.4 %all_gather.11 = f32[256,512]{0,1:T(8,128)} all-gather(f32[256,128]{0,1:T(8,128)} %reduce-scatter.6.cloned.1.call-done), channel_id=1, replica_groups=mesh['dp'=8,'col'=4] {'col'}, dimensions={1}, use_global_device_ids=true | all-gather | bytes 655360 | tf_op jit(solution)/shard_map/all_gather | solution.py:133
  183.4 42.8 %all-reduce.2.cloned.1.call-done.gram_ref = f32[512,512]{1,0:T(8,128)} async-done(((f32[512,512]{1,0:T(8,128)}), f32[512,512]{1,0:T(8,128)}) %all-reduce.2.cloned.1.call-update) | async-done | bytes 1048592 | tf_op jit(solution)/shard_map/psum | solution.py:129
  226.1 1.2 copy-done.1
  227.3 38.1 %shard_map.59 = f32[512,512]{1,0:T(8,128)S(1)} custom-call(f32[512,512]{1,0:T(8,128)S(1)} %copy-done.1), custom_call_target="tpu_custom_call" | custom-call | flops 1000000000 | bytes 2000000 | tf_op jit(solution)/shard_map/pallas_call | solution.py:74
  265.4 2.0 fusion.46
  267.4 1.9 fusion.7
  269.4 4.9 %add_convert_fusion = bf16[512,6656]{1,0:T(8,128)(2,1)} fusion(f32[512,6656]{1,0:T(8,128)S(1)} %fusion.7, bf16[256,6656]{1,0:T(8,128)(2,1)S(1)} %copy-done, f32[512,256]{1,0:T(8,128)S(1)} %fusion.46), kind=kOutput, calls=%fused_computation | convolution fusion | flops 1752170496 | bytes 24379392 | tf_op jit(solution)/shard_map/dot_general | solution.py:111
  274.3 2.0 copy.10
  276.4 61.4 %reduce-scatter.8.cloned.1.call-done = bf16[64,6656]{1,0:T(8,128)(2,1)} async-done(((bf16[512,6656]{1,0:T(8,128)(2,1)}), bf16[64,6656]{1,0:T(8,128)(2,1)}) %reduce-scatter.8.cloned.1.call-update) | async-done | bytes 851984 | tf_op jit(solution)/shard_map/reduce_scatter | solution.py:137
  337.8 2.5 convert_element_type.63
  (25 shorter events, 0.3 us)
Async XLA Ops:
  7.2 16.5 %copy-start = (bf16[256,6656]{1,0:T(8,128)(2,1)S(1)}, bf16[256,6656]{1,0:T(8,128)(2,1)}, u32[]{:S(2)}) copy-start(bf16[256,6656]{1,0:T(8,128)(2,1)} %param.5) | copy-start | bytes 10223620
  13.7 5.4 %copy-start.6 = (s32[8192]{0:T(1024)S(1)}, s32[8192]{0:T(1024)}, u32[]{:S(2)}) copy-start(s32[8192]{0:T(1024)} %param.6) | copy-start | bytes 98308
  13.7 5.4 %copy-start.7 = (s32[512]{0:T(512)S(1)}, s32[512]{0:T(512)}, u32[]{:S(2)}) copy-start(s32[512]{0:T(512)} %param.7) | copy-start | bytes 6148
  13.7 55.9 %all-to-all-start = ((bf16[256,8,1024]{0,2,1:T(8,128)(2,1)}), bf16[256,8,1024]{0,2,1:T(8,128)(2,1)}, u32[]{:S(2)}, u32[]{:S(2)}) async-start(bf16[256,8,1024]{0,2,1:T(8,128)(2,1)} %bitcast.27), calls=%async_computation.1 | async-start | bytes 8388608 | tf_op jit(solution)/shard_map/all_to_all | solution.py:121
  19.0 31.5 %reduce-scatter.4.cloned.1.call-start = ((), (), s32[]{:S(2)}) async-start(), calls=%async_computation.4 | async-start | bytes 655360 | tf_op jit(solution)/shard_map/reduce_scatter | solution.py:124
  26.5 49.6 %all-gather.3.cloned.1.call-start = ((), (), s32[]{:S(2)}) async-start(), calls=%async_computation.5 | async-start | bytes 1179648 | tf_op jit(solution)/shard_map/all_gather | solution.py:125
  50.6 77.6 %all-gather.5.cloned.1.call-start = ((), (), s32[]{:S(2)}) async-start(), calls=%async_computation.6 | async-start | bytes 2621440 | tf_op jit(solution)/shard_map/all_gather | solution.py:128
  76.1 3.7 %copy-start.2 = (bf16[8,256,1024]{2,1,0:T(8,128)(2,1)S(1)}, bf16[8,256,1024]{2,1,0:T(8,128)(2,1)}, u32[]{:S(2)}) copy-start(bf16[8,256,1024]{2,1,0:T(8,128)(2,1)} %copy.9) | copy-start | bytes 12582916
  76.1 4.0 %copy-start.5 = (f32[2048,128]{0,1:T(8,128)S(1)}, f32[2048,128]{0,1:T(8,128)}, u32[]{:S(2)}) copy-start(f32[2048,128]{0,1:T(8,128)} %all-gather.3.cloned.1.call-done) | copy-start | bytes 3145732
  81.8 84.2 %reduce-scatter.6.cloned.1.call-start = ((), (), s32[]{:S(2)}) async-start(), calls=%async_computation.8 | async-start | bytes 1179648 | tf_op jit(solution)/shard_map/reduce_scatter | solution.py:132
  81.8 4.0 %copy-start.3 = (bf16[8,256,1024]{2,1,0:T(8,128)(2,1)S(1)}, bf16[8,256,1024]{2,1,0:T(8,128)(2,1)}, u32[]{:S(2)}) copy-start(bf16[8,256,1024]{2,1,0:T(8,128)(2,1)} %copy.9) | copy-start | bytes 12582916
  81.8 4.0 %copy-start.4 = (f32[1024,128]{0,1:T(8,128)S(1)}, f32[1024,128]{0,1:T(8,128)}, u32[]{:S(2)}) copy-start(f32[1024,128]{0,1:T(8,128)} %fusion.2) | copy-start | bytes 1572868
  88.4 137.7 %all-reduce.2.cloned.1.call-start = ((), (), s32[]{:S(2)}) async-start(), calls=%async_computation.7 | async-start | bytes 2097152 | tf_op jit(solution)/shard_map/psum | solution.py:129
  134.9 202.9 %reduce-scatter.8.cloned.1.call-start = ((), (), s32[]{:S(2)}) async-start(), calls=%async_computation.9 | async-start | bytes 7667712 | tf_op jit(solution)/shard_map/reduce_scatter | solution.py:137
  226.1 1.2 copy-start.1
Sparse Core Ops, SparseCore 0:
  26.6 23.8 reduce-scatter.3
  52.4 23.5 all-gather.2
  81.9 46.1 all-gather.4
  131.2 34.7 reduce-scatter.5
  169.5 56.5 all-reduce.1
  274.4 63.2 reduce-scatter.7

commit v2 on v1

--- a/solution.py
+++ b/solution.py
@@ -1,3 +1,4 @@
+import functools
 import math
 
 import jax
@@ -83,6 +84,196 @@
     )(gram)
 
 
+MESH = pl.DeviceIdType.MESH
+SPACE = 48 * 1024 * 1024
+
+
+def others(axis, count, stride=1):
+    me = lax.axis_index(axis)
+    total = count * stride
+    for offset in range(1, count):
+        yield offset, lax.rem(me + offset * stride, total)
+
+
+def greet(groups):
+    barrier = pltpu.get_barrier_semaphore()
+    waits = 0
+    for axis, count, stride in groups:
+        for _, target in others(axis, count, stride):
+            pl.semaphore_signal(barrier, inc=1, device_id={axis: target}, device_id_type=MESH)
+            waits += 1
+    pl.semaphore_wait(barrier, waits)
+
+
+def send(source, target_ref, send_sem, recv_sem, axis, target):
+    copy = pltpu.make_async_remote_copy(
+        src_ref=source, dst_ref=target_ref, send_sem=send_sem, recv_sem=recv_sem,
+        device_id={axis: target}, device_id_type=MESH)
+    copy.start()
+    return copy
+
+
+def wait_all(copies):
+    for copy in copies:
+        copy.wait()
+
+
+def total_of(ref, count):
+    total = ref[0].astype(jnp.float32)
+    for index in range(1, count):
+        total = total + ref[index].astype(jnp.float32)
+    return total
+
+
+def first_kernel(n_dp, n_col, act_ref, part_ref, mine_ref, all_ref, landed, own, sa, ra, sc, rc, sd, rd, local_sem):
+    my_dp, my_col = lax.axis_index("dp"), lax.axis_index("col")
+    wide = mine_ref.shape[2]
+    greet([("dp", n_dp, 1), ("col", n_col, 1)])
+
+    def rows_of(device):
+        return act_ref.at[:, pl.ds(pl.multiple_of(device * wide, wide), wide)]
+
+    partial = [send(part_ref.at[target], landed.at[my_col], sc.at[k], rc.at[k], "col", target)
+               for k, target in others("col", n_col)]
+    rows = [send(rows_of(target), mine_ref.at[my_dp], sa.at[k], ra.at[k], "dp", target)
+            for k, target in others("dp", n_dp)]
+    kept_here = pltpu.make_async_copy(rows_of(my_dp), mine_ref.at[my_dp], local_sem)
+    kept_here.start()
+    landed[my_col] = part_ref[my_col]
+    wait_all(partial)
+    own[...] = total_of(landed, n_col).astype(own.dtype)
+    gathered = [send(own, all_ref.at[my_dp], sd.at[k], rd.at[k], "dp", target)
+                for k, target in others("dp", n_dp)]
+    all_ref[my_dp] = own[...]
+    wait_all(gathered)
+    kept_here.wait()
+    wait_all(rows)
+
+
+def first_exchange(activ, parts, n_dp, n_col):
+    tok, width = activ.shape
+    piece = parts.shape[1:]
+    dma = pltpu.SemaphoreType.DMA
+    return pl.pallas_call(
+        functools.partial(first_kernel, n_dp, n_col),
+        out_shape=(jax.ShapeDtypeStruct((n_dp, tok, width // n_dp), activ.dtype),
+                   jax.ShapeDtypeStruct((n_dp,) + piece, jnp.bfloat16)),
+        in_specs=[pl.BlockSpec(memory_space=pl.ANY), pl.BlockSpec(memory_space=pltpu.VMEM)],
+        out_specs=(pl.BlockSpec(memory_space=pl.ANY), pl.BlockSpec(memory_space=pltpu.VMEM)),
+        scratch_shapes=[pltpu.VMEM((n_col,) + piece, jnp.float32), pltpu.VMEM(piece, jnp.bfloat16),
+                        dma((n_dp,)), dma((n_dp,)), dma((n_col,)), dma((n_col,)),
+                        dma((n_dp,)), dma((n_dp,)), dma],
+        compiler_params=pltpu.CompilerParams(collective_id=0, has_side_effects=True, vmem_limit_bytes=SPACE),
+    )(activ, parts)
+
+
+def gram_kernel(n_dp, n_col, sketch_ref, back_ref, gram_ref, own_ref, rows, landed, part, gin, gcol,
+                ss, rs, sb, rb, s1, r1, s2, r2, s3, r3):
+    my_dp, my_col = lax.axis_index("dp"), lax.axis_index("col")
+    wide = sketch_ref.shape[1]
+    few = part.shape[1]
+    greet([("dp", n_dp, 1), ("col", n_col, 1)])
+    sketches = [send(sketch_ref, rows.at[my_col], ss.at[k], rs.at[k], "col", target)
+                for k, target in others("col", n_col)]
+    backs = [send(back_ref.at[target], landed.at[my_dp], sb.at[k], rb.at[k], "dp", target)
+             for k, target in others("dp", n_dp)]
+    rows[my_col] = sketch_ref[...]
+    landed[my_dp] = back_ref[my_dp]
+    wait_all(backs)
+    own_ref[...] = total_of(landed, n_dp)
+    wait_all(sketches)
+    mine = sketch_ref[...]
+    block = jnp.concatenate(
+        [lax.dot_general(mine, rows[c], (((0,), (0,)), ((), ())), preferred_element_type=jnp.float32)
+         for c in range(n_col)], axis=1)
+    for d in range(n_dp):
+        part[d] = block[d * few:(d + 1) * few, :]
+    parts = [send(part.at[target], gin.at[my_dp], s1.at[k], r1.at[k], "dp", target)
+             for k, target in others("dp", n_dp)]
+    gin[my_dp] = part[my_dp]
+    wait_all(parts)
+    gcol[my_col] = total_of(gin, n_dp)
+    spread = [send(gcol.at[my_col], gcol.at[my_col], s2.at[k], r2.at[k], "col", target)
+              for k, target in others("col", n_col)]
+    wait_all(spread)
+    full = [send(gcol, gram_ref.at[my_dp], s3.at[k], r3.at[k], "dp", target)
+            for k, target in others("dp", n_dp)]
+    gram_ref[my_dp] = gcol[...]
+    wait_all(full)
+
+
+def gram_exchange(sketch, back, n_dp, n_col):
+    rows, wide = sketch.shape
+    few = wide // n_dp
+    piece = back.shape[1:]
+    count = wide * n_col
+    dma = pltpu.SemaphoreType.DMA
+    vmem = pl.BlockSpec(memory_space=pltpu.VMEM)
+    gram, own = pl.pallas_call(
+        functools.partial(gram_kernel, n_dp, n_col),
+        out_shape=(jax.ShapeDtypeStruct((n_dp, n_col, few, count), jnp.float32),
+                   jax.ShapeDtypeStruct(piece, jnp.float32)),
+        in_specs=[vmem, vmem],
+        out_specs=(vmem, vmem),
+        scratch_shapes=[pltpu.VMEM((n_col, rows, wide), sketch.dtype), pltpu.VMEM((n_dp,) + piece, jnp.float32),
+                        pltpu.VMEM((n_dp, few, count), jnp.float32), pltpu.VMEM((n_dp, few, count), jnp.float32),
+                        pltpu.VMEM((n_col, few, count), jnp.float32),
+                        dma((n_col,)), dma((n_col,)), dma((n_dp,)), dma((n_dp,)), dma((n_dp,)), dma((n_dp,)),
+                        dma((n_col,)), dma((n_col,)), dma((n_dp,)), dma((n_dp,))],
+        compiler_params=pltpu.CompilerParams(collective_id=1, has_side_effects=True, vmem_limit_bytes=SPACE),
+    )(sketch, back)
+    return gram.transpose(1, 0, 2, 3).reshape(count, count), own
+
+
+def last_kernel(chips, tiles, left_ref, grad_ref, other_ref, out_ref, outgoing, landed, ss, rs):
+    my_dp = lax.axis_index("dp")
+    my_chip = my_dp // 2
+    half = grad_ref.shape[0]
+    rows = left_ref.shape[0] // 2
+    few = rows // chips
+    tile = grad_ref.shape[1] // tiles
+    greet([("dp", chips, 2)])
+    copies = []
+    for t in range(tiles):
+        at = pl.ds(t * tile, tile)
+        prod = (jnp.dot(left_ref[:, :half], grad_ref[:, at], preferred_element_type=jnp.float32)
+                + jnp.dot(left_ref[:, half:], other_ref[:, at], preferred_element_type=jnp.float32))
+        prod = prod[:rows] + prod[rows:]
+        for q in range(chips):
+            outgoing[t, q] = prod[q * few:(q + 1) * few].astype(outgoing.dtype)
+
+            @pl.when(my_chip == q)
+            def _(q=q):
+                out_ref[:, at] = prod[q * few:(q + 1) * few]
+
+        for k, target in others("dp", chips, 2):
+            copies.append((t, k, send(outgoing.at[t, target // 2], landed.at[t, k],
+                                      ss.at[t, k], rs.at[t, k], "dp", target)))
+    for t, k, copy in copies:
+        copy.wait()
+        at = pl.ds(t * tile, tile)
+        out_ref[:, at] = out_ref[:, at] + landed[t, k].astype(jnp.float32)
+
+
+def last_exchange(left, grad_out, other, chips):
+    width = grad_out.shape[1]
+    tiles = 4 if width % 512 == 0 else 1
+    tile = width // tiles
+    few = left.shape[0] // 2 // chips
+    dma = pltpu.SemaphoreType.DMA
+    vmem = pl.BlockSpec(memory_space=pltpu.VMEM)
+    return pl.pallas_call(
+        functools.partial(last_kernel, chips, tiles),
+        out_shape=jax.ShapeDtypeStruct((few, width), jnp.float32),
+        in_specs=[vmem, vmem, vmem],
+        out_specs=vmem,
+        scratch_shapes=[pltpu.VMEM((tiles, chips, few, tile), jnp.bfloat16),
+                        pltpu.VMEM((tiles, chips, few, tile), jnp.bfloat16),
+                        dma((tiles, chips)), dma((tiles, chips))],
+        compiler_params=pltpu.CompilerParams(collective_id=2, has_side_effects=True, vmem_limit_bytes=SPACE),
+    )(left, grad_out, other)
+
+
 def parity_sign(common, num_bits):
     parity = jnp.zeros_like(common)
     for shift_bit in range(num_bits):
@@ -117,26 +308,33 @@
     ff_dev = grad_out.shape[1]
     col_dev = signs.shape[0]
     total_cols = col_dev * col_count
-    highest = lax.Precision.HIGHEST
-    mine = lax.all_to_all(activ, "dp", split_axis=1, concat_axis=0, tiled=True)
+    dp_count = lax.axis_size("dp")
+    keep_count = kept.shape[0]
+    keep_col = keep_count // col_count
+    keep_dev = keep_count // dp_count
+    chips = dp_count // 2
+    tok_dev = activ.shape[0]
+    row_dev = activ.shape[1] // dp_count
+    my_core = lax.rem(lax.axis_index("dp"), 2)
+    swap = [(index, index ^ 1) for index in range(dp_count)]
+    grad_other = lax.ppermute(grad_out, "dp", swap)
     columns = kept_columns(signs, kept, my_col, ff_dev, col_dev, total_cols)
     mixed = dot_f32(grad_out, columns, ((1,), (0,))) * (1.0 / math.sqrt(total_cols))
-    mixed = lax.psum_scatter(mixed, "col", scatter_dimension=1, tiled=True)
-    mixed = lax.all_gather(mixed, "dp", axis=0, tiled=True)
-    top, rest = split(mixed)
-    sketch = dot_f32(mine, top, ((0,), (0,))) + dot_f32(mine, rest, ((0,), (0,)))
-    full_rows = lax.all_gather(sketch, "col", axis=1, tiled=True)
-    gram_matrix = lax.psum(jnp.dot(full_rows.T, full_rows, precision=highest), "dp")
+    mixed = mixed.reshape(tok_dev, col_count, keep_col).transpose(1, 0, 2)
+    mine, mixed = first_exchange(activ, mixed, dp_count, col_count)
+    mine = mine.reshape(dp_count * tok_dev, row_dev)
+    mixed = mixed.reshape(dp_count * tok_dev, keep_col)
+    sketch = dot_f32(mine, mixed, ((0,), (0,)))
     top, rest = split(sketch)
     back = dot_f32(mine, top, ((1,), (0,))) + dot_f32(mine, rest, ((1,), (0,)))
-    back = lax.psum_scatter(back, "dp", scatter_dimension=0, tiled=True)
+    gram_matrix, back = gram_exchange(top, back.reshape(dp_count, tok_dev, keep_col), dp_count, col_count)
     back = lax.all_gather(back, "col", axis=1, tiled=True)
-    solved = dot_hi(inverse_factor(gram_matrix), back, ((1,), (1,)))
-    top, rest = split(solved)
-    part = dot_f32(top, grad_out, ((1,), (0,))) + dot_f32(rest, grad_out, ((1,), (0,)))
-    projection = lax.psum_scatter(
-        part.astype(jnp.bfloat16), "dp", scatter_dimension=0, tiled=True
-    ).astype(jnp.float32)
+    back = jnp.concatenate([back, lax.ppermute(back, "dp", swap)], axis=0)
+    inverse = inverse_factor(gram_matrix).reshape(chips, 2, keep_dev, keep_count)
+    inverse = lax.dynamic_index_in_dim(inverse, my_core, 1, keepdims=False)
+    solved = dot_hi(inverse.reshape(chips * keep_dev, keep_count), back, ((1,), (1,)))
+    left = jnp.concatenate(split(solved), axis=0)
+    projection = last_exchange(left, grad_out, grad_other, chips)
     return (sketch, projection)
 
 

time: 348 us -> 231 us (0.66)
  waiting for transfers between devices: 218 us -> 0.01 us
  Pallas kernels: 38.1 us -> 188 us
  matrix products: 29.8 us -> 8.89 us
  between operations: 14.3 us -> 0.78 us
  local copies, waits for them, and re-layouts: 17 us -> 8.8 us
  starting transfers between devices: 5.72 us -> 0.52 us
    pallas_call x0 -> x3, Pallas kernels: none -> 150 us  [the longest x1 57.4 us: first_exchange(): pl.pallas_call(functools.partial(first_kernel, n_dp, n_col), out_shape=(j...]
    reduce_scatter x3 -> x0, waiting for transfers between devices: 116 us -> none  [the longest x1 61.4 us: per_device(): lax.psum_scatter(part.astype(jnp.bfloat16), 'dp', scatter_dimension=0, ti...]
    psum x1 -> x0, waiting for transfers between devices: 42.8 us -> none  [per_device(): lax.psum(jnp.dot(full_rows.T, full_rows, precision=highest), 'dp')]
    all_gather x2 -> x0, waiting for transfers between devices: 39.5 us -> none  [the longest x1 39.5 us: per_device(): full_rows = lax.all_gather(sketch, 'col', axis=1, tiled=True)]
    all_to_all x1 -> x0, waiting for transfers between devices: 19.1 us -> none  [per_device(): mine = lax.all_to_all(activ, 'dp', split_axis=1, concat_axis=0, tiled=True)]
    dot_general x7 -> x4, matrix products: 21.1 us -> 6.63 us  [dot_f32(): lax.dot_general(left, right, (dims, ((), ())), preferred_element_type=jnp...]
    dot_general x1 -> x0, matrix products: 6.71 us -> none  [per_device(): jnp.dot(full_rows.T, full_rows, precision=highest)]
    all_to_all x1 -> x0, local copies, waits for them, and re-layouts: 6.46 us -> none  [per_device(): mine = lax.all_to_all(activ, 'dp', split_axis=1, concat_axis=0, tiled=True)]
  transfers between devices with their start and end apart: 7 -> 2, of which waited for: 6 -> 0; matrix products, arithmetic and copies ran while one was open for 8% -> 9% of each run, Pallas kernels for 0% -> 62%
where the time goes in v2:
time: 231 us; the launch traced here: 230 us
  Pallas kernels  188 us (81%)
  blocking collectives  16.9 us (7%)
  matrix products  8.89 us (4%)
  local copies, waits for them, and re-layouts  8.8 us (4%)
  other arithmetic  6.66 us (3%)
    pallas_call x1, Pallas kernels, first_exchange(): pl.pallas_call(functools.partial(first_kernel, n_dp, n_col), out_shape=(j...  57.4 us
    pallas_call x1, Pallas kernels, gram_exchange(): pl.pallas_call(functools.partial(gram_kernel, n_dp, n_col), out_shape=(ja...  47.6 us
    pallas_call x1, Pallas kernels, last_exchange(): pl.pallas_call(functools.partial(last_kernel, chips, tiles), out_shape=ja...  44.6 us
    pallas_call x1, Pallas kernels, inverse_factor(): pl.pallas_call(inverse_factor_kernel, out_shape=jax.ShapeDtypeStruct((cou...  38.1 us
    all_gather x1, blocking collectives, per_device(): back = lax.all_gather(back, 'col', axis=1, tiled=True)  16.9 us
    dot_general x4, matrix products, dot_f32(): lax.dot_general(left, right, (dims, ((), ())), preferred_element_type=jnp...  6.63 us
  transfers between devices with their start and end apart: 2, of which 0 were waited for; matrix products, arithmetic and copies ran while one was open for 9% of the time, Pallas kernels for 62%

profile of v2, /device:TPU:0, one launch (start us, length us, event | category | flops | bytes accessed | tf_op | source)
XLA Modules:
  0.0 230.3 jit_solution(1347952273785753400)
XLA Ops:
  0.6 0.5 collective-permute-start.1
  1.2 1.1 subtract_convert_fusion.3
  2.3 0.9 fusion.36
  3.2 0.8 slice_convert_fusion
  3.9 0.4 broadcast_multiply_fusion
  4.4 0.0 copy-start
  4.4 3.4 %bitcast_multiply_fusion = bf16[6656,512]{1,0:T(8,128)(2,1)S(1)} fusion(bf16[52,128,512]{2,1,0:T(8,128)(2,1)S(1)} %broadcast_multiply_fusion, bf16[6656]{0:T(1024)(128)(2,1)S(1)} %slice_convert_fusion), kind=kLoop, calls=%fused_computation | loop fusion | flops 3407872 | bytes 13644800 | tf_op jit(solution)/shard_map/mul | solution.py:293
  7.8 0.0 copy-done
  7.8 2.8 %convolution_multiply_fusion = f32[512,256]{1,0:T(8,128)} fusion(bf16[6656,512]{1,0:T(8,128)(2,1)S(1)} %bitcast_multiply_fusion, bf16[256,6656]{1,0:T(8,128)(2,1)S(1)} %copy-done), kind=kOutput, calls=%fused_computation.3 | convolution fusion | flops 1744961536 | bytes 10747904 | tf_op jit(solution)/shard_map/dot_general | solution.py:302
  10.6 2.0 copy.8
  12.6 0.0 copy-start.1
  12.6 1.0 copy-done.1
  13.7 57.4 %shard_map.59 = (bf16[8,256,1024]{2,1,0:T(8,128)(2,1)S(1)}, bf16[8,256,128]{2,1,0:T(8,128)(2,1)S(1)}) custom-call(bf16[256,8192]{1,0:T(8,128)(2,1)} %act_ref.1, f32[4,256,128]{2,1,0:T(8,128)S(1)} %bitcast.25), custom_call_target="tpu_custom_call" | custom-call | tf_op jit(solution)/shard_map/pallas_call | solution.py:157
  71.1 1.3 fusion.38
  72.4 0.0 copy-start.4
  72.4 1.3 fusion.39
  73.7 1.3 convolution_add_fusion
  75.0 0.0 copy-done.4
  75.0 47.6 %shard_map.60 = (f32[8,4,16,512]{3,2,1,0:T(8,128)S(1)}, f32[256,128]{1,0:T(8,128)S(1)}) custom-call(bf16[1024,128]{1,0:T(8,128)(2,1)S(1)} %get-tuple-element.12.sketch_ref, f32[8,256,128]{2,1,0:T(8,128)S(1)} %bitcast.24), custom_call_target="tpu_custom_call" | custom-call | tf_op jit(solution)/shard_map/pallas_call | solution.py:212
  122.6 0.0 copy-start.2
  122.6 1.0 copy-done.2
  123.6 16.9 %all_gather.3 = f32[256,512]{1,0:T(8,128)} all-gather(f32[256,128]{1,0:T(8,128)S(1)} %get-tuple-element.9), channel_id=1, replica_groups=mesh['dp'=8,'col'=4] {'col'}, dimensions={1}, use_global_device_ids=true | all-gather | bytes 655360 | tf_op jit(solution)/shard_map/all_gather | solution.py:331
  140.5 0.0 collective-permute-start
  140.5 2.3 copy.10
  142.8 0.0 copy-start.3
  142.8 1.2 copy-done.3
  144.0 38.1 %shard_map.61 = f32[512,512]{1,0:T(8,128)S(1)} custom-call(f32[512,512]{1,0:T(8,128)S(1)} %bitcast.27), custom_call_target="tpu_custom_call" | custom-call | flops 1000000000 | bytes 2000000 | tf_op jit(solution)/shard_map/pallas_call | solution.py:75
  182.1 0.0 collective-permute-done
  182.1 2.3 subtract_convert_fusion
  184.4 0.0 collective-permute-done.1.other_ref
  184.4 44.6 %shard_map.62 = f32[64,6656]{1,0:T(8,128)S(1)} custom-call(bf16[512,512]{1,0:T(8,128)(2,1)S(1)} %pad_maximum_fusion.left_ref, bf16[256,6656]{1,0:T(8,128)(2,1)S(1)} %copy-done, bf16[256,6656]{1,0:T(8,128)(2,1)} %collective-permute-done.1.other_ref), custom_call_target="tpu_custom_call" | custom-call | tf_op jit(solution)/shard_map/pallas_call | solution.py:265
  229.1 1.2 copy.13
  (3 shorter events, 0.1 us)
Async XLA Ops:
  0.6 183.8 %collective-permute-start.1 = (bf16[256,6656]{1,0:T(8,128)(2,1)}, bf16[256,6656]{1,0:T(8,128)(2,1)}, u32[]{:S(2)}, u32[]{:S(2)}) collective-permute-start(bf16[256,6656]{1,0:T(8,128)(2,1)} %grad_ref.1), channel_id=1, source_target_pairs={{0,4},{4,0},{8,12},{12,8},{16,20},{20,16},{24,28},{28,24},{1,5},{5... | collective-permute-start | bytes 10223624 | tf_op jit(solution)/shard_map/ppermute | solution.py:320
  4.4 3.4 %copy-start = (bf16[256,6656]{1,0:T(8,128)(2,1)S(1)}, bf16[256,6656]{1,0:T(8,128)(2,1)}, u32[]{:S(2)}) copy-start(bf16[256,6656]{1,0:T(8,128)(2,1)} %grad_ref.1) | copy-start | bytes 10223620
  12.6 1.0 copy-start.1
  72.4 2.6 %copy-start.4 = (f32[1024,128]{1,0:T(8,128)}, f32[1024,128]{1,0:T(8,128)S(1)}, u32[]{:S(2)}) copy-start(f32[1024,128]{1,0:T(8,128)S(1)} %get-tuple-element.16) | copy-start | bytes 1572868
  122.6 1.0 copy-start.2
  140.5 41.6 %collective-permute-start = (f32[256,512]{1,0:T(8,128)}, f32[256,512]{1,0:T(8,128)}, u32[]{:S(2)}, u32[]{:S(2)}) collective-permute-start(f32[256,512]{1,0:T(8,128)} %all_gather.3), channel_id=1, source_target_pairs={{0,4},{4,0},{8,12},{12,8},{16,20},{20,16},{24,28},{28,24},{1,5},{5... | collective-permute-start | bytes 1572872 | tf_op jit(solution)/shard_map/ppermute | solution.py:332
  142.8 1.2 copy-start.3

commit v3 on v2

--- a/solution.py
+++ b/solution.py
@@ -14,6 +14,22 @@
 def dot_hi(left, right, dims):
     return lax.dot_general(left, right, (dims, ((), ())), precision=HI,
                            preferred_element_type=jnp.float32)
+
+
+def thirds(values):
+    top = values.astype(jnp.bfloat16).astype(jnp.float32)
+    rest = values - top
+    mid = rest.astype(jnp.bfloat16).astype(jnp.float32)
+    return top, mid, rest - mid
+
+
+def outer_sum(left, right):
+    la, lb, lc = thirds(left)
+    ra, rb, rc = thirds(right)
+    return lax.dot_general(
+        jnp.concatenate([la, la, lb, lb, la, lc], axis=0).astype(jnp.bfloat16),
+        jnp.concatenate([ra, rb, ra, rb, rc, ra], axis=0).astype(jnp.bfloat16),
+        (((0,), (0,)), ((), ())), preferred_element_type=jnp.float32)
 
 
 def factor_block(both_ref):
@@ -37,8 +53,7 @@
         done = jnp.concatenate([rw, rv], axis=1)
         both_ref[lo:lo + 8, :] = done
         if lo + 8 < size:
-            left = jnp.where(lane >= lo + 8, rw, 0.0)
-            step = dot_hi(left, done, ((0,), (0,)))
+            step = outer_sum(jnp.where(lane >= lo + 8, rw, 0.0), done)
             both_ref[lo + 8:, :] = both_ref[lo + 8:, :] - step[lo + 8:, :]
 
 
@@ -80,7 +95,7 @@
         scratch_shapes=[pltpu.VMEM((count, count), jnp.float32),
                         pltpu.VMEM((size, 2 * size), jnp.float32)],
         compiler_params=pltpu.CompilerParams(vmem_limit_bytes=32 * 1024 * 1024),
-        cost_estimate=pl.CostEstimate(flops=10**9, bytes_accessed=2 * 10**6, transcendentals=4096),
+        cost_estimate=pl.CostEstimate(flops=4 * 10**10, bytes_accessed=2 * 10**6, transcendentals=4096),
     )(gram)
 
 
@@ -125,49 +140,56 @@
     return total
 
 
-def first_kernel(n_dp, n_col, act_ref, part_ref, mine_ref, all_ref, landed, own, sa, ra, sc, rc, sd, rd, local_sem):
+def first_kernel(n_dp, n_col, act_ref, part_ref, out_ref, landed, outgoing, arrived, sc, rc, sd, rd):
     my_dp, my_col = lax.axis_index("dp"), lax.axis_index("col")
-    wide = mine_ref.shape[2]
+    wide = out_ref.shape[0]
     greet([("dp", n_dp, 1), ("col", n_col, 1)])
-
-    def rows_of(device):
-        return act_ref.at[:, pl.ds(pl.multiple_of(device * wide, wide), wide)]
-
     partial = [send(part_ref.at[target], landed.at[my_col], sc.at[k], rc.at[k], "col", target)
                for k, target in others("col", n_col)]
-    rows = [send(rows_of(target), mine_ref.at[my_dp], sa.at[k], ra.at[k], "dp", target)
-            for k, target in others("dp", n_dp)]
-    kept_here = pltpu.make_async_copy(rows_of(my_dp), mine_ref.at[my_dp], local_sem)
-    kept_here.start()
     landed[my_col] = part_ref[my_col]
     wait_all(partial)
-    own[...] = total_of(landed, n_col).astype(own.dtype)
-    gathered = [send(own, all_ref.at[my_dp], sd.at[k], rd.at[k], "dp", target)
-                for k, target in others("dp", n_dp)]
-    all_ref[my_dp] = own[...]
-    wait_all(gathered)
-    kept_here.wait()
-    wait_all(rows)
+    mixed = total_of(landed, n_col)
+    width = mixed.shape[1]
+    top = mixed.astype(jnp.bfloat16)
+    rest = (mixed - top.astype(jnp.float32)).astype(jnp.bfloat16)
+    both = jnp.concatenate([top, rest], axis=1)
+
+    def rows_of(device):
+        rows = act_ref[:, pl.ds(pl.multiple_of(device * wide, wide), wide)]
+        prod = lax.dot_general(rows, both, (((0,), (0,)), ((), ())), preferred_element_type=jnp.float32)
+        return prod[:, :width] + prod[:, width:]
+
+    copies = []
+    for k, target in others("dp", n_dp):
+        outgoing[k] = rows_of(target).astype(outgoing.dtype)
+        copies.append(send(outgoing.at[k], arrived.at[k], sd.at[k], rd.at[k], "dp", target))
+    out_ref[...] = rows_of(my_dp)
+    wait_all(copies)
+    total = out_ref[...]
+    for k in range(1, n_dp):
+        total = total + arrived[k].astype(jnp.float32)
+    out_ref[...] = total
 
 
 def first_exchange(activ, parts, n_dp, n_col):
-    tok, width = activ.shape
+    wide = activ.shape[1] // n_dp
     piece = parts.shape[1:]
     dma = pltpu.SemaphoreType.DMA
+    vmem = pl.BlockSpec(memory_space=pltpu.VMEM)
     return pl.pallas_call(
         functools.partial(first_kernel, n_dp, n_col),
-        out_shape=(jax.ShapeDtypeStruct((n_dp, tok, width // n_dp), activ.dtype),
-                   jax.ShapeDtypeStruct((n_dp,) + piece, jnp.bfloat16)),
-        in_specs=[pl.BlockSpec(memory_space=pl.ANY), pl.BlockSpec(memory_space=pltpu.VMEM)],
-        out_specs=(pl.BlockSpec(memory_space=pl.ANY), pl.BlockSpec(memory_space=pltpu.VMEM)),
-        scratch_shapes=[pltpu.VMEM((n_col,) + piece, jnp.float32), pltpu.VMEM(piece, jnp.bfloat16),
-                        dma((n_dp,)), dma((n_dp,)), dma((n_col,)), dma((n_col,)),
-                        dma((n_dp,)), dma((n_dp,)), dma],
+        out_shape=jax.ShapeDtypeStruct((wide, piece[1]), jnp.float32),
+        in_specs=[vmem, vmem],
+        out_specs=vmem,
+        scratch_shapes=[pltpu.VMEM((n_col,) + piece, jnp.float32),
+                        pltpu.VMEM((n_dp, wide, piece[1]), jnp.bfloat16),
+                        pltpu.VMEM((n_dp, wide, piece[1]), jnp.bfloat16),
+                        dma((n_col,)), dma((n_col,)), dma((n_dp,)), dma((n_dp,))],
         compiler_params=pltpu.CompilerParams(collective_id=0, has_side_effects=True, vmem_limit_bytes=SPACE),
     )(activ, parts)
 
 
-def gram_kernel(n_dp, n_col, sketch_ref, back_ref, gram_ref, own_ref, rows, landed, part, gin, gcol,
+def gram_kernel(n_dp, n_col, sketch_ref, gram_ref, all_ref, rows, part, gin, gcol,
                 ss, rs, sb, rb, s1, r1, s2, r2, s3, r3):
     my_dp, my_col = lax.axis_index("dp"), lax.axis_index("col")
     wide = sketch_ref.shape[1]
@@ -175,12 +197,10 @@
     greet([("dp", n_dp, 1), ("col", n_col, 1)])
     sketches = [send(sketch_ref, rows.at[my_col], ss.at[k], rs.at[k], "col", target)
                 for k, target in others("col", n_col)]
-    backs = [send(back_ref.at[target], landed.at[my_dp], sb.at[k], rb.at[k], "dp", target)
-             for k, target in others("dp", n_dp)]
+    shared = [send(sketch_ref, all_ref.at[my_dp], sb.at[k], rb.at[k], "dp", target)
+              for k, target in others("dp", n_dp)]
     rows[my_col] = sketch_ref[...]
-    landed[my_dp] = back_ref[my_dp]
-    wait_all(backs)
-    own_ref[...] = total_of(landed, n_dp)
+    all_ref[my_dp] = sketch_ref[...]
     wait_all(sketches)
     mine = sketch_ref[...]
     block = jnp.concatenate(
@@ -200,29 +220,29 @@
             for k, target in others("dp", n_dp)]
     gram_ref[my_dp] = gcol[...]
     wait_all(full)
-
-
-def gram_exchange(sketch, back, n_dp, n_col):
+    wait_all(shared)
+
+
+def gram_exchange(sketch, n_dp, n_col):
     rows, wide = sketch.shape
     few = wide // n_dp
-    piece = back.shape[1:]
     count = wide * n_col
     dma = pltpu.SemaphoreType.DMA
     vmem = pl.BlockSpec(memory_space=pltpu.VMEM)
-    gram, own = pl.pallas_call(
+    gram, gathered = pl.pallas_call(
         functools.partial(gram_kernel, n_dp, n_col),
         out_shape=(jax.ShapeDtypeStruct((n_dp, n_col, few, count), jnp.float32),
-                   jax.ShapeDtypeStruct(piece, jnp.float32)),
-        in_specs=[vmem, vmem],
+                   jax.ShapeDtypeStruct((n_dp, rows, wide), sketch.dtype)),
+        in_specs=[vmem],
         out_specs=(vmem, vmem),
-        scratch_shapes=[pltpu.VMEM((n_col, rows, wide), sketch.dtype), pltpu.VMEM((n_dp,) + piece, jnp.float32),
+        scratch_shapes=[pltpu.VMEM((n_col, rows, wide), sketch.dtype),
                         pltpu.VMEM((n_dp, few, count), jnp.float32), pltpu.VMEM((n_dp, few, count), jnp.float32),
                         pltpu.VMEM((n_col, few, count), jnp.float32),
                         dma((n_col,)), dma((n_col,)), dma((n_dp,)), dma((n_dp,)), dma((n_dp,)), dma((n_dp,)),
                         dma((n_col,)), dma((n_col,)), dma((n_dp,)), dma((n_dp,))],
         compiler_params=pltpu.CompilerParams(collective_id=1, has_side_effects=True, vmem_limit_bytes=SPACE),
-    )(sketch, back)
-    return gram.transpose(1, 0, 2, 3).reshape(count, count), own
+    )(sketch)
+    return gram.transpose(1, 0, 2, 3).reshape(count, count), gathered.reshape(n_dp * rows, wide)
 
 
 def last_kernel(chips, tiles, left_ref, grad_ref, other_ref, out_ref, outgoing, landed, ss, rs):
@@ -314,22 +334,23 @@
     keep_dev = keep_count // dp_count
     chips = dp_count // 2
     tok_dev = activ.shape[0]
-    row_dev = activ.shape[1] // dp_count
     my_core = lax.rem(lax.axis_index("dp"), 2)
     swap = [(index, index ^ 1) for index in range(dp_count)]
+    act_other = lax.ppermute(activ, "dp", swap)
     grad_other = lax.ppermute(grad_out, "dp", swap)
     columns = kept_columns(signs, kept, my_col, ff_dev, col_dev, total_cols)
     mixed = dot_f32(grad_out, columns, ((1,), (0,))) * (1.0 / math.sqrt(total_cols))
     mixed = mixed.reshape(tok_dev, col_count, keep_col).transpose(1, 0, 2)
-    mine, mixed = first_exchange(activ, mixed, dp_count, col_count)
-    mine = mine.reshape(dp_count * tok_dev, row_dev)
-    mixed = mixed.reshape(dp_count * tok_dev, keep_col)
-    sketch = dot_f32(mine, mixed, ((0,), (0,)))
-    top, rest = split(sketch)
-    back = dot_f32(mine, top, ((1,), (0,))) + dot_f32(mine, rest, ((1,), (0,)))
-    gram_matrix, back = gram_exchange(top, back.reshape(dp_count, tok_dev, keep_col), dp_count, col_count)
-    back = lax.all_gather(back, "col", axis=1, tiled=True)
-    back = jnp.concatenate([back, lax.ppermute(back, "dp", swap)], axis=0)
+    sketch = first_exchange(activ, mixed, dp_count, col_count)
+    gram_matrix, rounded = gram_exchange(sketch.astype(jnp.bfloat16), dp_count, col_count)
+    own = dot_f32(jnp.concatenate([activ, act_other], axis=0), rounded, ((1,), (0,)))
+    back = jnp.zeros((2 * tok_dev, keep_count), jnp.float32)
+    for offset in range(col_count):
+        piece = own
+        if offset:
+            piece = lax.ppermute(own, "col", [(c, (c + offset) % col_count) for c in range(col_count)])
+        place = lax.rem(my_col - offset + col_count, col_count) * keep_col
+        back = lax.dynamic_update_slice(back, piece, (0, place))
     inverse = inverse_factor(gram_matrix).reshape(chips, 2, keep_dev, keep_count)
     inverse = lax.dynamic_index_in_dim(inverse, my_core, 1, keepdims=False)
     solved = dot_hi(inverse.reshape(chips * keep_dev, keep_count), back, ((1,), (1,)))

time: 231 us -> 199 us (0.86)
  Pallas kernels: 188 us -> 161 us
  blocking collectives: 16.9 us -> 0 us
  starting transfers between devices: 0.52 us -> 5.77 us
  waiting for transfers between devices: 0.01 us -> 5.12 us
    pallas_call x1, Pallas kernels: 57.4 us -> 39.3 us  [first_exchange(): pl.pallas_call(functools.partial(first_kernel, n_dp, n_col), out_shape=ja...]
    all_gather x1 -> x0, blocking collectives: 16.9 us -> none  [per_device(): back = lax.all_gather(back, 'col', axis=1, tiled=True)]
    pallas_call x1, Pallas kernels: 38.1 us -> 26.6 us  [inverse_factor(): pl.pallas_call(inverse_factor_kernel, out_shape=jax.ShapeDtypeStruct((cou...]
    ppermute x1 -> x4, starting transfers between devices: 0.01 us -> 5.69 us  [the longest x3 5.17 us: per_device(): lax.ppermute(own, 'col', [(c, (c + offset) % col_count) for c in range(co...]
    ppermute x1 -> x4, waiting for transfers between devices: 0.01 us -> 5.12 us  [the longest x3 5.11 us: per_device(): lax.ppermute(own, 'col', [(c, (c + offset) % col_count) for c in range(co...]
    pallas_call x1, Pallas kernels: 47.6 us -> 51 us  [gram_exchange(): pl.pallas_call(functools.partial(gram_kernel, n_dp, n_col), out_shape=(ja...]
    dot_general x4 -> x2, matrix products: 6.63 us -> 8.39 us  [dot_f32(): lax.dot_general(left, right, (dims, ((), ())), preferred_element_type=jnp...]
    unnamed x11 -> x12, local copies, waits for them, and re-layouts: 4.43 us -> 5.59 us
  transfers between devices with their start and end apart: 2 -> 5, of which waited for: 0 -> 1; matrix products, arithmetic and copies ran while one was open for 9% -> 10% of each run, Pallas kernels for 62% -> 59%
where the time goes in v3:
time: 199 us
  Pallas kernels  161 us (81%)
  matrix products  10.7 us (5%)
  local copies, waits for them, and re-layouts  8.16 us (4%)
  other arithmetic  6.68 us (3%)
  starting transfers between devices  5.77 us (3%)
  waiting for transfers between devices  5.12 us (3%)
    pallas_call x1, Pallas kernels, gram_exchange(): pl.pallas_call(functools.partial(gram_kernel, n_dp, n_col), out_shape=(ja...  51 us
    pallas_call x1, Pallas kernels, last_exchange(): pl.pallas_call(functools.partial(last_kernel, chips, tiles), out_shape=ja...  44.4 us
    pallas_call x1, Pallas kernels, first_exchange(): pl.pallas_call(functools.partial(first_kernel, n_dp, n_col), out_shape=ja...  39.3 us
    pallas_call x1, Pallas kernels, inverse_factor(): pl.pallas_call(inverse_factor_kernel, out_shape=jax.ShapeDtypeStruct((cou...  26.6 us
    dot_general x2, matrix products, dot_f32(): lax.dot_general(left, right, (dims, ((), ())), preferred_element_type=jnp...  8.39 us
    unnamed x12, local copies, waits for them, and re-layouts  5.59 us
    ppermute x3, starting transfers between devices, per_device(): lax.ppermute(own, 'col', [(c, (c + offset) % col_count) for c in range(co...  5.17 us
    ppermute x3, waiting for transfers between devices, per_device(): lax.ppermute(own, 'col', [(c, (c + offset) % col_count) for c in range(co...  5.11 us
  transfers between devices with their start and end apart: 5, of which 1 were waited for; matrix products, arithmetic and copies ran while one was open for 10% of the time, Pallas kernels for 59%

profile of v3, /device:TPU:0, one launch (start us, length us, event | category | flops | bytes accessed | tf_op | source)
XLA Modules:
  0.0 198.6 jit_solution(8090314499000578649)
XLA Ops:
  0.6 0.5 collective-permute-start
  1.1 0.1 collective-permute-start.4
  1.2 0.8 slice_convert_fusion
  2.0 0.9 fusion.36
  2.9 1.1 subtract_convert_fusion.1
  4.0 0.4 broadcast_multiply_fusion
  4.5 0.0 copy-start.1
  4.5 3.4 %bitcast_multiply_fusion = bf16[6656,512]{1,0:T(8,128)(2,1)S(1)} fusion(bf16[52,128,512]{2,1,0:T(8,128)(2,1)S(1)} %broadcast_multiply_fusion, bf16[6656]{0:T(1024)(128)(2,1)S(1)} %slice_convert_fusion), kind=kLoop, calls=%fused_computation.4 | loop fusion | flops 3407872 | bytes 13644800 | tf_op jit(solution)/shard_map/mul | solution.py:313
  7.9 2.0 %convolution_multiply_fusion = f32[512,256]{1,0:T(8,128)S(1)} fusion(bf16[6656,512]{1,0:T(8,128)(2,1)S(1)} %bitcast_multiply_fusion, bf16[256,6656]{1,0:T(8,128)(2,1)S(1)} %copy-done.1), kind=kOutput, calls=%fused_computation.6 | convolution fusion | flops 1744961536 | bytes 10747904 | tf_op jit(solution)/shard_map/dot_general | solution.py:322
  9.9 0.2 copy.7
  10.1 0.0 copy-start
  10.1 2.2 %copy-done = bf16[256,8192]{1,0:T(8,128)(2,1)S(1)} copy-done((bf16[256,8192]{1,0:T(8,128)(2,1)S(1)}, bf16[256,8192]{1,0:T(8,128)(2,1)}, u32[]{:S(2)}) %copy-start) | copy-done | bytes 4194328
  12.3 39.3 %shard_map.59 = f32[1024,128]{1,0:T(8,128)S(1)} custom-call(bf16[256,8192]{1,0:T(8,128)(2,1)S(1)} %copy-done, f32[4,256,128]{2,1,0:T(8,128)S(1)} %bitcast.16), custom_call_target="tpu_custom_call" | custom-call | tf_op jit(solution)/shard_map/pallas_call | solution.py:179
  51.7 51.0 %shard_map.60 = (f32[8,4,16,512]{3,2,1,0:T(8,128)S(1)}, bf16[8,1024,128]{2,1,0:T(8,128)(2,1)S(1)}) custom-call(bf16[1024,128]{1,0:T(8,128)(2,1)S(1)} %convert_element_type.32.sketch_ref), custom_call_target="tpu_custom_call" | custom-call | tf_op jit(solution)/shard_map/pallas_call | solution.py:232
  102.7 1.4 copy-done.3
  104.1 0.1 copy.8
  104.2 0.1 broadcast_in_dim.2
  104.3 6.4 %constant_dynamic-update-slice_fusion.3 = (f32[512,512]{1,0:T(8,128)S(1)}, f32[512,128]{1,0:T(8,128)S(1)}) fusion(f32[512,512]{1,0:T(8,128)S(1)} %broadcast_in_dim.2, s32[]{:T(128)S(6)} %select_n.17, bf16[8192,128]{1,0:T(8,128)(2,1)} %bitcast.20, bf16[256,8192]{1,0:T(8,128)(2,1)} %collective-permute-done, bf16[256,8192]{1,0:T(8,128)(2,1)} %act_ref.1), kind=kOutput, calls=%fused_computation.62 | convolution fusion | flops 1090519040 | bytes 11010052 | tf_op jit(solution)/shard_map/dot_general | solution.py:322
  110.7 0.0 copy-start.4
  110.7 1.5 collective-permute-start.1
  112.2 1.4 collective-permute-start.2
  113.6 26.6 %shard_map.61 = f32[512,512]{1,0:T(8,128)S(1)} custom-call(f32[512,512]{1,0:T(8,128)S(1)} %bitcast.17), custom_call_target="tpu_custom_call" | custom-call | flops 40000000000 | bytes 2000000 | tf_op jit(solution)/shard_map/pallas_call | solution.py:90
  140.3 2.3 %collective-permute-start.3 = (f32[512,128]{1,0:T(8,128)S(1)}, f32[512,128]{1,0:T(8,128)S(1)}, u32[]{:S(2)}, u32[]{:S(2)}) collective-permute-start(f32[512,128]{1,0:T(8,128)S(1)} %get-tuple-element.9), channel_id=1, source_target_pairs={{0,3},{1,0},{2,1},{3,2},{4,7},{5,4},{6,5},{7,6},{8,11},{9,8},{10,9... | collective-permute-start | bytes 786440 | tf_op jit(solution)/shard_map/ppermute | solution.py:351
  142.6 0.0 copy-start.2
  142.6 0.7 constant_dynamic-update-slice_fusion.2
  143.4 0.7 constant_dynamic-update-slice_fusion.1
  144.1 5.1 %collective-permute-done.3 = f32[512,128]{1,0:T(8,128)S(1)} collective-permute-done((f32[512,128]{1,0:T(8,128)S(1)}, f32[512,128]{1,0:T(8,128)S(1)}, u32[]{:S(2)}, u32[]{:S(2)}) %collective-permute-start.3) | collective-permute-done | bytes 262176 | tf_op jit(solution)/shard_map/ppermute | solution.py:351
  149.2 0.7 constant_dynamic-update-slice_fusion
  149.9 2.3 %subtract_convert_fusion = (bf16[256,512]{1,0:T(8,128)(2,1)S(1)}, bf16[256,512]{1,0:T(8,128)(2,1)S(1)}) fusion(f32[256,512]{1,0:T(8,128)S(1)} %bitcast.21, f32[512,512]{1,0:T(8,128)} %constant_dynamic-update-slice_fusion), kind=kOutput, calls=%fused_computation.23 | convolution fusion | flops 805830656 | bytes 2097152 | tf_op jit(solution)/shard_map/dot_general | solution.py:15
  152.3 44.4 %shard_map.62 = f32[64,6656]{1,0:T(8,128)S(1)} custom-call(bf16[512,512]{1,0:T(8,128)(2,1)S(1)} %pad_maximum_fusion.left_ref, bf16[256,6656]{1,0:T(8,128)(2,1)S(1)} %copy-done.2, bf16[256,6656]{1,0:T(8,128)(2,1)} %collective-permute-done.4.other_ref), custom_call_target="tpu_custom_call" | custom-call | tf_op jit(solution)/shard_map/pallas_call | solution.py:285
  196.7 0.8 copy.15
  197.5 1.2 copy.16
  (12 shorter events, 0.1 us)
Async XLA Ops:
  0.6 103.6 %collective-permute-start = (bf16[256,8192]{1,0:T(8,128)(2,1)}, bf16[256,8192]{1,0:T(8,128)(2,1)}, u32[]{:S(2)}, u32[]{:S(2)}) collective-permute-start(bf16[256,8192]{1,0:T(8,128)(2,1)} %act_ref.1), channel_id=1, source_target_pairs={{0,4},{4,0},{8,12},{12,8},{16,20},{20,16},{24,28},{28,24},{1,5},{5... | collective-permute-start | bytes 12582920 | tf_op jit(solution)/shard_map/ppermute | solution.py:339
  1.1 151.1 %collective-permute-start.4 = (bf16[256,6656]{1,0:T(8,128)(2,1)}, bf16[256,6656]{1,0:T(8,128)(2,1)}, u32[]{:S(2)}, u32[]{:S(2)}) collective-permute-start(bf16[256,6656]{1,0:T(8,128)(2,1)} %grad_ref.1), channel_id=1, source_target_pairs={{0,4},{4,0},{8,12},{12,8},{16,20},{20,16},{24,28},{28,24},{1,5},{5... | collective-permute-start | bytes 10223624 | tf_op jit(solution)/shard_map/ppermute | solution.py:340
  4.5 3.4 %copy-start.1 = (bf16[256,6656]{1,0:T(8,128)(2,1)S(1)}, bf16[256,6656]{1,0:T(8,128)(2,1)}, u32[]{:S(2)}) copy-start(bf16[256,6656]{1,0:T(8,128)(2,1)} %grad_ref.1) | copy-start | bytes 10223620
  10.1 2.2 %copy-start = (bf16[256,8192]{1,0:T(8,128)(2,1)S(1)}, bf16[256,8192]{1,0:T(8,128)(2,1)}, u32[]{:S(2)}) copy-start(bf16[256,8192]{1,0:T(8,128)(2,1)} %act_ref.1) | copy-start | bytes 12582916
  102.7 1.4 copy-start.3
  110.7 2.9 %copy-start.4 = (f32[512,512]{1,0:T(8,128)}, f32[512,512]{1,0:T(8,128)S(1)}, u32[]{:S(2)}) copy-start(f32[512,512]{1,0:T(8,128)S(1)} %get-tuple-element.8) | copy-start | bytes 3145732
  110.7 31.9 %collective-permute-start.1 = (f32[512,128]{1,0:T(8,128)S(1)}, f32[512,128]{1,0:T(8,128)S(1)}, u32[]{:S(2)}, u32[]{:S(2)}) collective-permute-start(f32[512,128]{1,0:T(8,128)S(1)} %get-tuple-element.9), channel_id=1, source_target_pairs={{0,1},{1,2},{2,3},{3,0},{4,5},{5,6},{6,7},{7,4},{8,9},{9,10},{10,1... | collective-permute-start | bytes 786440 | tf_op jit(solution)/shard_map/ppermute | solution.py:351
  112.2 31.1 %collective-permute-start.2 = (f32[512,128]{1,0:T(8,128)S(1)}, f32[512,128]{1,0:T(8,128)S(1)}, u32[]{:S(2)}, u32[]{:S(2)}) collective-permute-start(f32[512,128]{1,0:T(8,128)S(1)} %get-tuple-element.9), channel_id=1, source_target_pairs={{0,2},{1,3},{2,0},{3,1},{4,6},{5,7},{6,4},{7,5},{8,10},{9,11},{10,... | collective-permute-start | bytes 786440 | tf_op jit(solution)/shard_map/ppermute | solution.py:351
  140.3 8.9 %collective-permute-start.3 = (f32[512,128]{1,0:T(8,128)S(1)}, f32[512,128]{1,0:T(8,128)S(1)}, u32[]{:S(2)}, u32[]{:S(2)}) collective-permute-start(f32[512,128]{1,0:T(8,128)S(1)} %get-tuple-element.9), channel_id=1, source_target_pairs={{0,3},{1,0},{2,1},{3,2},{4,7},{5,4},{6,5},{7,6},{8,11},{9,8},{10,9... | collective-permute-start | bytes 786440 | tf_op jit(solution)/shard_map/ppermute | solution.py:351
  142.6 9.6 %copy-start.2 = (bf16[256,6656]{1,0:T(8,128)(2,1)S(1)}, bf16[256,6656]{1,0:T(8,128)(2,1)}, u32[]{:S(2)}) copy-start(bf16[256,6656]{1,0:T(8,128)(2,1)} %grad_ref.1) | copy-start | bytes 10223620

commit v4 on v3

--- a/solution.py
+++ b/solution.py
@@ -133,6 +133,24 @@
         copy.wait()
 
 
+def gather_pairs(source, target_ref, count, sems):
+    s1, r1, s2, r2 = sems
+    me = lax.axis_index("dp")
+    partner = me + 1 - 2 * lax.rem(me, 2)
+    first = [(k, send(source, target_ref.at[me], s1.at[k], r1.at[k], "dp", target))
+             for k, target in others("dp", count // 2, 2)]
+    second = [send(source, target_ref.at[me], s2.at[0], r2.at[0], "dp", partner)]
+
+    def finish():
+        for k, copy in first:
+            copy.wait()
+            origin = lax.rem(me - 2 * k + count, count)
+            second.append(send(target_ref.at[origin], target_ref.at[origin], s2.at[k], r2.at[k], "dp", partner))
+        wait_all(second)
+
+    return finish
+
+
 def total_of(ref, count):
     total = ref[0].astype(jnp.float32)
     for index in range(1, count):
@@ -181,7 +199,7 @@
         out_shape=jax.ShapeDtypeStruct((wide, piece[1]), jnp.float32),
         in_specs=[vmem, vmem],
         out_specs=vmem,
-        scratch_shapes=[pltpu.VMEM((n_col,) + piece, jnp.float32),
+        scratch_shapes=[pltpu.VMEM((n_col,) + piece, jnp.bfloat16),
                         pltpu.VMEM((n_dp, wide, piece[1]), jnp.bfloat16),
                         pltpu.VMEM((n_dp, wide, piece[1]), jnp.bfloat16),
                         dma((n_col,)), dma((n_col,)), dma((n_dp,)), dma((n_dp,))],
@@ -190,15 +208,14 @@
 
 
 def gram_kernel(n_dp, n_col, sketch_ref, gram_ref, all_ref, rows, part, gin, gcol,
-                ss, rs, sb, rb, s1, r1, s2, r2, s3, r3):
+                ss, rs, sb, rb, s1, r1, s2, r2, s3, r3, sf, rf, s4, r4):
     my_dp, my_col = lax.axis_index("dp"), lax.axis_index("col")
     wide = sketch_ref.shape[1]
     few = part.shape[1]
     greet([("dp", n_dp, 1), ("col", n_col, 1)])
     sketches = [send(sketch_ref, rows.at[my_col], ss.at[k], rs.at[k], "col", target)
                 for k, target in others("col", n_col)]
-    shared = [send(sketch_ref, all_ref.at[my_dp], sb.at[k], rb.at[k], "dp", target)
-              for k, target in others("dp", n_dp)]
+    shared = gather_pairs(sketch_ref, all_ref, n_dp, (sb, rb, sf, rf))
     rows[my_col] = sketch_ref[...]
     all_ref[my_dp] = sketch_ref[...]
     wait_all(sketches)
@@ -216,11 +233,10 @@
     spread = [send(gcol.at[my_col], gcol.at[my_col], s2.at[k], r2.at[k], "col", target)
               for k, target in others("col", n_col)]
     wait_all(spread)
-    full = [send(gcol, gram_ref.at[my_dp], s3.at[k], r3.at[k], "dp", target)
-            for k, target in others("dp", n_dp)]
+    full = gather_pairs(gcol, gram_ref, n_dp, (s3, r3, s4, r4))
     gram_ref[my_dp] = gcol[...]
-    wait_all(full)
-    wait_all(shared)
+    shared()
+    full()
 
 
 def gram_exchange(sketch, n_dp, n_col):
@@ -239,7 +255,8 @@
                         pltpu.VMEM((n_dp, few, count), jnp.float32), pltpu.VMEM((n_dp, few, count), jnp.float32),
                         pltpu.VMEM((n_col, few, count), jnp.float32),
                         dma((n_col,)), dma((n_col,)), dma((n_dp,)), dma((n_dp,)), dma((n_dp,)), dma((n_dp,)),
-                        dma((n_col,)), dma((n_col,)), dma((n_dp,)), dma((n_dp,))],
+                        dma((n_col,)), dma((n_col,)), dma((n_dp,)), dma((n_dp,)),
+                        dma((n_dp,)), dma((n_dp,)), dma((n_dp,)), dma((n_dp,))],
         compiler_params=pltpu.CompilerParams(collective_id=1, has_side_effects=True, vmem_limit_bytes=SPACE),
     )(sketch)
     return gram.transpose(1, 0, 2, 3).reshape(count, count), gathered.reshape(n_dp * rows, wide)
@@ -341,7 +358,7 @@
     columns = kept_columns(signs, kept, my_col, ff_dev, col_dev, total_cols)
     mixed = dot_f32(grad_out, columns, ((1,), (0,))) * (1.0 / math.sqrt(total_cols))
     mixed = mixed.reshape(tok_dev, col_count, keep_col).transpose(1, 0, 2)
-    sketch = first_exchange(activ, mixed, dp_count, col_count)
+    sketch = first_exchange(activ, mixed.astype(jnp.bfloat16), dp_count, col_count)
     gram_matrix, rounded = gram_exchange(sketch.astype(jnp.bfloat16), dp_count, col_count)
     own = dot_f32(jnp.concatenate([activ, act_other], axis=0), rounded, ((1,), (0,)))
     back = jnp.zeros((2 * tok_dev, keep_count), jnp.float32)

time: 199 us -> 188 us (0.945)
  Pallas kernels: 161 us -> 151 us
    pallas_call x1, Pallas kernels: 39.3 us -> 34.2 us  [first_exchange(): pl.pallas_call(functools.partial(first_kernel, n_dp, n_col), out_shape=ja...]
    pallas_call x1, Pallas kernels: 51 us -> 47.3 us  [gram_exchange(): pl.pallas_call(functools.partial(gram_kernel, n_dp, n_col), out_shape=(ja...]
  transfers between devices with their start and end apart: 5 -> 5, of which waited for: 1 -> 1; matrix products, arithmetic and copies ran while one was open for 10% -> 11% of each run, Pallas kernels for 59% -> 58%
where the time goes in v4:
time: 188 us
  Pallas kernels  151 us (80%)
  matrix products  10.7 us (6%)
  local copies, waits for them, and re-layouts  8.14 us (4%)
  other arithmetic  6.68 us (4%)
  starting transfers between devices  5.69 us (3%)
  waiting for transfers between devices  4.33 us (2%)
    pallas_call x1, Pallas kernels, gram_exchange(): pl.pallas_call(functools.partial(gram_kernel, n_dp, n_col), out_shape=(ja...  47.3 us
    pallas_call x1, Pallas kernels, last_exchange(): pl.pallas_call(functools.partial(last_kernel, chips, tiles), out_shape=ja...  43.3 us
    pallas_call x1, Pallas kernels, first_exchange(): pl.pallas_call(functools.partial(first_kernel, n_dp, n_col), out_shape=ja...  34.2 us
    pallas_call x1, Pallas kernels, inverse_factor(): pl.pallas_call(inverse_factor_kernel, out_shape=jax.ShapeDtypeStruct((cou...  26.6 us
    dot_general x2, matrix products, dot_f32(): lax.dot_general(left, right, (dims, ((), ())), preferred_element_type=jnp...  8.4 us
    unnamed x12, local copies, waits for them, and re-layouts  5.59 us
    ppermute x3, starting transfers between devices, per_device(): lax.ppermute(own, 'col', [(c, (c + offset) % col_count) for c in range(co...  5.09 us
    ppermute x3, waiting for transfers between devices, per_device(): lax.ppermute(own, 'col', [(c, (c + offset) % col_count) for c in range(co...  4.33 us
  transfers between devices with their start and end apart: 5, of which 1 were waited for; matrix products, arithmetic and copies ran while one was open for 11% of the time, Pallas kernels for 58%

profile of v4, /device:TPU:0, one launch (start us, length us, event | category | flops | bytes accessed | tf_op | source)
XLA Modules:
  0.0 187.8 jit_solution(16293960563605522745)
XLA Ops:
  0.6 0.5 collective-permute-start
  1.1 0.1 collective-permute-start.4
  1.2 0.8 slice_convert_fusion
  2.0 0.9 fusion.37
  2.9 1.1 subtract_convert_fusion.1
  4.0 0.4 broadcast_multiply_fusion
  4.5 0.0 copy-start.1
  4.5 3.4 %bitcast_multiply_fusion = bf16[6656,512]{1,0:T(8,128)(2,1)S(1)} fusion(bf16[52,128,512]{2,1,0:T(8,128)(2,1)S(1)} %broadcast_multiply_fusion, bf16[6656]{0:T(1024)(128)(2,1)S(1)} %slice_convert_fusion), kind=kLoop, calls=%fused_computation.4 | loop fusion | flops 3407872 | bytes 13644800 | tf_op jit(solution)/shard_map/mul | solution.py:330
  7.9 2.0 %fusion.4 = bf16[512,256]{1,0:T(8,128)(2,1)S(1)} fusion(bf16[6656,512]{1,0:T(8,128)(2,1)S(1)} %bitcast_multiply_fusion, bf16[256,6656]{1,0:T(8,128)(2,1)S(1)} %copy-done.1), kind=kOutput, calls=%fused_computation.7 | convolution fusion | flops 1745092608 | bytes 10485760 | tf_op jit(solution)/shard_map/dot_general | solution.py:339
  9.9 0.2 copy.7
  10.1 0.0 copy-start
  10.1 2.2 %copy-done = bf16[256,8192]{1,0:T(8,128)(2,1)S(1)} copy-done((bf16[256,8192]{1,0:T(8,128)(2,1)S(1)}, bf16[256,8192]{1,0:T(8,128)(2,1)}, u32[]{:S(2)}) %copy-start) | copy-done | bytes 4194328
  12.3 34.2 %shard_map.59 = f32[1024,128]{1,0:T(8,128)S(1)} custom-call(bf16[256,8192]{1,0:T(8,128)(2,1)S(1)} %copy-done, bf16[4,256,128]{2,1,0:T(8,128)(2,1)S(1)} %bitcast.16), custom_call_target="tpu_custom_call" | custom-call | tf_op jit(solution)/shard_map/pallas_call | solution.py:197
  46.5 47.3 %shard_map.60 = (f32[8,4,16,512]{3,2,1,0:T(8,128)S(1)}, bf16[8,1024,128]{2,1,0:T(8,128)(2,1)S(1)}) custom-call(bf16[1024,128]{1,0:T(8,128)(2,1)S(1)} %convert_element_type.45.sketch_ref), custom_call_target="tpu_custom_call" | custom-call | tf_op jit(solution)/shard_map/pallas_call | solution.py:248
  93.8 1.4 copy-done.3
  95.2 0.1 copy.8
  95.3 0.1 broadcast_in_dim.2
  95.5 6.4 %constant_dynamic-update-slice_fusion.3 = (f32[512,512]{1,0:T(8,128)S(1)}, f32[512,128]{1,0:T(8,128)S(1)}) fusion(f32[512,512]{1,0:T(8,128)S(1)} %broadcast_in_dim.2, s32[]{:T(128)S(6)} %select_n.17, bf16[8192,128]{1,0:T(8,128)(2,1)} %bitcast.20, bf16[256,8192]{1,0:T(8,128)(2,1)} %collective-permute-done, bf16[256,8192]{1,0:T(8,128)(2,1)} %act_ref.1), kind=kOutput, calls=%fused_computation.63 | convolution fusion | flops 1090519040 | bytes 11010052 | tf_op jit(solution)/shard_map/dot_general | solution.py:339
  101.9 0.0 copy-start.4
  101.9 1.4 collective-permute-start.1
  103.3 0.9 collective-permute-start.2
  104.2 26.6 %shard_map.61 = f32[512,512]{1,0:T(8,128)S(1)} custom-call(f32[512,512]{1,0:T(8,128)S(1)} %bitcast.17), custom_call_target="tpu_custom_call" | custom-call | flops 40000000000 | bytes 2000000 | tf_op jit(solution)/shard_map/pallas_call | solution.py:90
  130.8 2.8 %collective-permute-start.3 = (f32[512,128]{1,0:T(8,128)S(1)}, f32[512,128]{1,0:T(8,128)S(1)}, u32[]{:S(2)}, u32[]{:S(2)}) collective-permute-start(f32[512,128]{1,0:T(8,128)S(1)} %get-tuple-element.9), channel_id=1, source_target_pairs={{0,3},{1,0},{2,1},{3,2},{4,7},{5,4},{6,5},{7,6},{8,11},{9,8},{10,9... | collective-permute-start | bytes 786440 | tf_op jit(solution)/shard_map/ppermute | solution.py:368
  133.7 0.0 copy-start.2
  133.7 0.7 constant_dynamic-update-slice_fusion.2
  134.4 0.7 constant_dynamic-update-slice_fusion.1
  135.1 4.3 %collective-permute-done.3 = f32[512,128]{1,0:T(8,128)S(1)} collective-permute-done((f32[512,128]{1,0:T(8,128)S(1)}, f32[512,128]{1,0:T(8,128)S(1)}, u32[]{:S(2)}, u32[]{:S(2)}) %collective-permute-start.3) | collective-permute-done | bytes 262176 | tf_op jit(solution)/shard_map/ppermute | solution.py:368
  139.5 0.7 constant_dynamic-update-slice_fusion
  140.2 2.3 %subtract_convert_fusion = (bf16[256,512]{1,0:T(8,128)(2,1)S(1)}, bf16[256,512]{1,0:T(8,128)(2,1)S(1)}) fusion(f32[256,512]{1,0:T(8,128)S(1)} %bitcast.21, f32[512,512]{1,0:T(8,128)} %constant_dynamic-update-slice_fusion), kind=kOutput, calls=%fused_computation.24 | convolution fusion | flops 805830656 | bytes 2097152 | tf_op jit(solution)/shard_map/dot_general | solution.py:15
  142.5 43.3 %shard_map.62 = f32[64,6656]{1,0:T(8,128)S(1)} custom-call(bf16[512,512]{1,0:T(8,128)(2,1)S(1)} %pad_maximum_fusion.left_ref, bf16[256,6656]{1,0:T(8,128)(2,1)S(1)} %copy-done.2, bf16[256,6656]{1,0:T(8,128)(2,1)} %collective-permute-done.4.other_ref), custom_call_target="tpu_custom_call" | custom-call | tf_op jit(solution)/shard_map/pallas_call | solution.py:302
  185.8 0.8 copy.15
  186.6 1.2 copy.16
  (12 shorter events, 0.1 us)
Async XLA Ops:
  0.6 94.7 %collective-permute-start = (bf16[256,8192]{1,0:T(8,128)(2,1)}, bf16[256,8192]{1,0:T(8,128)(2,1)}, u32[]{:S(2)}, u32[]{:S(2)}) collective-permute-start(bf16[256,8192]{1,0:T(8,128)(2,1)} %act_ref.1), channel_id=1, source_target_pairs={{0,4},{4,0},{8,12},{12,8},{16,20},{20,16},{24,28},{28,24},{1,5},{5... | collective-permute-start | bytes 12582920 | tf_op jit(solution)/shard_map/ppermute | solution.py:356
  1.1 141.4 %collective-permute-start.4 = (bf16[256,6656]{1,0:T(8,128)(2,1)}, bf16[256,6656]{1,0:T(8,128)(2,1)}, u32[]{:S(2)}, u32[]{:S(2)}) collective-permute-start(bf16[256,6656]{1,0:T(8,128)(2,1)} %grad_ref.1), channel_id=1, source_target_pairs={{0,4},{4,0},{8,12},{12,8},{16,20},{20,16},{24,28},{28,24},{1,5},{5... | collective-permute-start | bytes 10223624 | tf_op jit(solution)/shard_map/ppermute | solution.py:357
  4.5 3.4 %copy-start.1 = (bf16[256,6656]{1,0:T(8,128)(2,1)S(1)}, bf16[256,6656]{1,0:T(8,128)(2,1)}, u32[]{:S(2)}) copy-start(bf16[256,6656]{1,0:T(8,128)(2,1)} %grad_ref.1) | copy-start | bytes 10223620
  10.1 2.2 %copy-start = (bf16[256,8192]{1,0:T(8,128)(2,1)S(1)}, bf16[256,8192]{1,0:T(8,128)(2,1)}, u32[]{:S(2)}) copy-start(bf16[256,8192]{1,0:T(8,128)(2,1)} %act_ref.1) | copy-start | bytes 12582916
  93.8 1.4 copy-start.3
  101.9 2.3 %copy-start.4 = (f32[512,512]{1,0:T(8,128)}, f32[512,512]{1,0:T(8,128)S(1)}, u32[]{:S(2)}) copy-start(f32[512,512]{1,0:T(8,128)S(1)} %get-tuple-element.8) | copy-start | bytes 3145732
  101.9 31.8 %collective-permute-start.1 = (f32[512,128]{1,0:T(8,128)S(1)}, f32[512,128]{1,0:T(8,128)S(1)}, u32[]{:S(2)}, u32[]{:S(2)}) collective-permute-start(f32[512,128]{1,0:T(8,128)S(1)} %get-tuple-element.9), channel_id=1, source_target_pairs={{0,1},{1,2},{2,3},{3,0},{4,5},{5,6},{6,7},{7,4},{8,9},{9,10},{10,1... | collective-permute-start | bytes 786440 | tf_op jit(solution)/shard_map/ppermute | solution.py:368
  103.3 31.1 %collective-permute-start.2 = (f32[512,128]{1,0:T(8,128)S(1)}, f32[512,128]{1,0:T(8,128)S(1)}, u32[]{:S(2)}, u32[]{:S(2)}) collective-permute-start(f32[512,128]{1,0:T(8,128)S(1)} %get-tuple-element.9), channel_id=1, source_target_pairs={{0,2},{1,3},{2,0},{3,1},{4,6},{5,7},{6,4},{7,5},{8,10},{9,11},{10,... | collective-permute-start | bytes 786440 | tf_op jit(solution)/shard_map/ppermute | solution.py:368
  130.8 8.7 %collective-permute-start.3 = (f32[512,128]{1,0:T(8,128)S(1)}, f32[512,128]{1,0:T(8,128)S(1)}, u32[]{:S(2)}, u32[]{:S(2)}) collective-permute-start(f32[512,128]{1,0:T(8,128)S(1)} %get-tuple-element.9), channel_id=1, source_target_pairs={{0,3},{1,0},{2,1},{3,2},{4,7},{5,4},{6,5},{7,6},{8,11},{9,8},{10,9... | collective-permute-start | bytes 786440 | tf_op jit(solution)/shard_map/ppermute | solution.py:368
  133.7 8.9 %copy-start.2 = (bf16[256,6656]{1,0:T(8,128)(2,1)S(1)}, bf16[256,6656]{1,0:T(8,128)(2,1)}, u32[]{:S(2)}) copy-start(bf16[256,6656]{1,0:T(8,128)(2,1)} %grad_ref.1) | copy-start | bytes 10223620
